TPU v7x, 256 devices: a whole 4x4x8 slice. The times are simulated.
256 devices in a mesh: ctx: 32 (over z, x_hi, core), chan: 8 (over y, x_lo).
Axes of the slice: x: 4 (x_hi: 2, x_lo: 2; x = x_hi * 2 + x_lo), y: 4, z: 8, core: 2. Of those that a mesh axis runs over, the one named last changes fastest.
Arguments:
- queries: bfloat16 [4096, 4096], P('ctx', 'chan'), may hold values from -6 to 6
- key_input: bfloat16 [4096, 4096], P('ctx', 'chan'), may hold values from -6 to 6
- gate_values: bfloat16 [4096, 4096], P('ctx', 'chan'), may hold values from -6 to 6
- cotangent: bfloat16 [4096, 4096], P('ctx', 'chan'), may hold values from -6 to 6
- out_weight: bfloat16 [4096, 4096], P('chan', 'ctx'), may hold values from -0.09375 to 0.09375
- decay_rates: float32 [4096, 16], P('chan'), may hold values from 2.4414062e-06 to 0.033
- residues: float32 [4096, 16], P('chan'), may hold values from -1.5 to 1.5
- skip_gain: float32 [4096], P('chan'), may hold values from 0.5 to 1.5
Outputs:
- final: bfloat16 [4096, 4096], P('ctx', 'chan')
- grad_queries: bfloat16 [4096, 4096], P('ctx', 'chan')
- grad_keys: bfloat16 [4096, 4096], P('ctx', 'chan')
- grad_gates: bfloat16 [4096, 4096], P('ctx', 'chan')
- grad_weight: bfloat16 [4096, 4096], P('chan', 'ctx')
- grad_residues: float32 [4096, 16], P('chan')
- grad_skip: float32 [4096], P('chan')
All inputs are finite; a program needn't handle non-finite values.
Results may differ from a plain program's by a relative error of at most 0.013.
Values may be sent and summed in bfloat16 or wider, within the bound.
A program may use at most 128 MiB of HBM per device.

v0:
```python
import math

import jax
import jax.numpy as jnp
from jax import lax
from jax.sharding import PartitionSpec as P

block_len = 32
highest = lax.Precision.HIGHEST


def combine_pair(earlier, later):
    return (earlier[0] * later[0], later[0] * earlier[1] + later[1])


def mode_gain(rates, residue_rows, length):
    twice = -2.0 * rates
    norms = jnp.sqrt(jnp.expm1(twice * length) / jnp.expm1(twice))
    return (residue_rows / norms, norms)


def local_pass(signal, rates, gains):
    positions, chans = signal.shape
    block_count = positions // block_len
    blocks = signal.reshape(block_count, block_len, chans)
    steps = jnp.arange(block_len, dtype=jnp.float32)
    decay_table = jnp.exp(-rates[None] * steps[:, None, None])
    filter_taps = jnp.einsum("dcm,cm->dc", decay_table, gains, precision=highest)
    lag_table = steps[:, None] - steps[None, :]
    onehot = (lag_table[:, :, None] == steps[None, None, :]).astype(jnp.float32)
    toeplitz = jnp.einsum("tsd,dc->tsc", onehot, filter_taps, precision=highest)
    inner_part = jnp.einsum("tsc,bsc->btc", toeplitz, blocks, precision=highest)
    tail_decay = jnp.flip(decay_table, 0)
    block_ends = jnp.einsum("bsc,scm->bcm", blocks, tail_decay, precision=highest)
    factors = jnp.broadcast_to(jnp.exp(-rates * block_len)[None], block_ends.shape)
    running = lax.associative_scan(combine_pair, (factors, block_ends), axis=0)[1]
    before = jnp.concatenate([jnp.zeros_like(running[:1]), running[:-1]], axis=0)
    return (inner_part, before, running[-1], decay_table)


def finish(inner_part, before, carry, rates, gains, decay_table):
    block_count = before.shape[0]
    block_index = jnp.arange(block_count, dtype=jnp.float32)
    carried = jnp.exp(-rates[None] * (block_len * block_index)[:, None, None]) * carry[None]
    states = before + carried
    lead_decay = decay_table * jnp.exp(-rates)[None] * gains[None]
    cross_part = jnp.einsum("bcm,tcm->btc", states, lead_decay, precision=highest)
    return ((inner_part + cross_part).reshape(block_count * block_len, -1), states)


def mode_grad(signal, conv_grad, states, rates, decay_table):
    positions, chans = signal.shape
    block_count = positions // block_len
    blocks = signal.reshape(block_count, block_len, chans)
    grad_blocks = conv_grad.reshape(block_count, block_len, chans)
    lead_plain = decay_table * jnp.exp(-rates)[None]
    weighted = jnp.einsum("btc,tcm->bcm", grad_blocks, lead_plain, precision=highest)
    cross_part = jnp.sum(states * weighted, axis=0)
    steps = jnp.arange(block_len, dtype=jnp.float32)
    lower = (steps[:, None] >= steps[None, :]).astype(jnp.float32)

    def one_mode(mode_rate):
        grow_table = jnp.exp(mode_rate[None] * steps[:, None])
        shrink = jnp.exp(-mode_rate[None] * steps[:, None])
        cumulated = jnp.einsum("ts,bsc->btc", lower, blocks * grow_table[None], precision=highest)
        return jnp.sum(grad_blocks * shrink[None] * cumulated, axis=(0, 1))

    local_part = lax.map(one_mode, rates.T).T
    return cross_part + local_part


def shards(
    queries, key_input, gate_values, cotangent, out_weight, decay_rates, residues, skip_gain
):
    positions = queries.shape[0]
    length = positions * lax.axis_size("ctx")
    scale = 1.0 / math.sqrt(length)
    full_rows = lax.all_gather(cotangent, "chan", axis=1, tiled=True)
    whole_weight = lax.all_gather(out_weight, "ctx", axis=1, tiled=True)
    query_cols, key_cols, gate_cols = (
        lax.all_to_all(queries, "ctx", split_axis=1, concat_axis=0, tiled=True),
        lax.all_to_all(key_input, "ctx", split_axis=1, concat_axis=0, tiled=True),
        lax.all_to_all(gate_values, "ctx", split_axis=1, concat_axis=0, tiled=True),
    )
    part = query_cols.shape[1]
    offset = lax.axis_index("ctx") * part
    rate_part = lax.dynamic_slice_in_dim(decay_rates, offset, part, 0)
    residue_part = lax.dynamic_slice_in_dim(residues, offset, part, 0)
    skip_part = lax.dynamic_slice_in_dim(skip_gain, offset, part, 0)
    gains, norms = mode_gain(rate_part, residue_part, length)
    query_f = query_cols.astype(jnp.float32)
    key_f = key_cols.astype(jnp.float32)
    gate_f = gate_cols.astype(jnp.float32)
    gated = query_f * key_f
    inner_part, before, device_end, decay_table = local_pass(gated, rate_part, gains)
    conv_out, states = finish(
        inner_part, before, jnp.zeros_like(device_end), rate_part, gains, decay_table
    )
    conv_out = conv_out + skip_part[None, :] * gated
    mixed_cols = (gate_f * conv_out).astype(jnp.bfloat16)
    mixed = lax.all_to_all(mixed_cols, "ctx", split_axis=0, concat_axis=1, tiled=True)
    partial_out = jnp.dot(mixed, whole_weight, preferred_element_type=jnp.float32)
    final = lax.psum_scatter(partial_out, "chan", scatter_dimension=1, tiled=True).astype(
        jnp.bfloat16
    )
    out_grad = lax.dot_general(
        full_rows, whole_weight, (((1,), (1,)), ((), ())), preferred_element_type=jnp.float32
    ).astype(jnp.bfloat16)
    weight_term = lax.dot_general(
        mixed, full_rows, (((0,), (0,)), ((), ())), preferred_element_type=jnp.float32
    )
    grad_weight = (
        lax.psum_scatter(weight_term, "ctx", scatter_dimension=1, tiled=True) * scale
    ).astype(jnp.bfloat16)
    grad_cols = lax.all_to_all(out_grad, "ctx", split_axis=1, concat_axis=0, tiled=True)
    conv_grad = grad_cols.astype(jnp.float32) * gate_f
    inner_back, before_back, end_back, unused_table = local_pass(
        jnp.flip(conv_grad, 0), rate_part, gains
    )
    back_conv = finish(
        inner_back, before_back, jnp.zeros_like(end_back), rate_part, gains, decay_table
    )[0]
    gated_grad = jnp.flip(back_conv, 0) + skip_part[None, :] * conv_grad
    query_grad = (gated_grad * key_f).astype(jnp.bfloat16)
    key_grad = (gated_grad * query_f).astype(jnp.bfloat16)
    gate_grad = (grad_cols.astype(jnp.float32) * conv_out).astype(jnp.bfloat16)
    grad_queries, grad_keys, grad_gates = (
        lax.all_to_all(query_grad, "ctx", split_axis=0, concat_axis=1, tiled=True),
        lax.all_to_all(key_grad, "ctx", split_axis=0, concat_axis=1, tiled=True),
        lax.all_to_all(gate_grad, "ctx", split_axis=0, concat_axis=1, tiled=True),
    )
    residue_terms = mode_grad(gated, conv_grad, states, rate_part, decay_table) / norms
    skip_terms = jnp.sum(conv_grad * gated, axis=0)
    residue_sum, skip_sum = (
        lax.all_gather(residue_terms, "ctx", axis=0, tiled=True),
        lax.all_gather(skip_terms, "ctx", axis=0, tiled=True),
    )
    return (
        final,
        grad_queries,
        grad_keys,
        grad_gates,
        grad_weight,
        residue_sum * scale,
        skip_sum * scale,
    )


def solution(mesh):
    placed = (
        P("ctx", "chan"),
        P("ctx", "chan"),
        P("ctx", "chan"),
        P("ctx", "chan"),
        P("chan", "ctx"),
        P("chan", None),
        P("chan", None),
        P("chan"),
    )
    return jax.shard_map(
        shards,
        mesh=mesh,
        in_specs=placed,
        out_specs=(
            P("ctx", "chan"),
            P("ctx", "chan"),
            P("ctx", "chan"),
            P("ctx", "chan"),
            P("chan", "ctx"),
            P("chan", None),
            P("chan"),
        ),
        check_vma=False,
    )
```

profile of v0, /device:TPU:8, one launch (start us, length us, event | category | flops | bytes accessed | tf_op | source)
XLA Modules:
  0.0 697.6 jit_solution(1139461798148943299)
XLA Ops:
  10.3 11.3 %all-to-all-start.2 = ((bf16[128,32,16]{0,2,1:T(8,128)(2,1)}), bf16[128,32,16]{0,2,1:T(8,128)(2,1)S(1)}, u32[]{:S(2)}, u32[]{:S(2)}) async-start(bf16[128,32,16]{0,2,1:T(8,128)(2,1)} %bitcast.3), calls=%async_computation.2 | async-start | bytes 262144 | tf_op jit(solution)/shard_map/all_to_all | solution.py:82
  24.8 7.6 %all-to-all-done.2 = bf16[128,32,16]{0,2,1:T(8,128)(2,1)S(1)} async-done(((bf16[128,32,16]{0,2,1:T(8,128)(2,1)}), bf16[128,32,16]{0,2,1:T(8,128)(2,1)S(1)}, u32[]{:S(2)}, u32[]{:S(2)}) %all-to-all-start.2) | async-done | bytes 131104 | tf_op jit(solution)/shard_map/all_to_all | solution.py:82
  32.4 3.9 all-to-all-start.1
  42.9 4.1 all-to-all-done.1
  47.0 5.7 all-to-all-start
  55.0 90.2 %all-gather.3.cloned.1.call-done = bf16[512,4096]{1,0:T(8,128)(2,1)} async-done(((bf16[512,128]{1,0:T(8,128)(2,1)}), bf16[512,4096]{1,0:T(8,128)(2,1)}) %all-gather.3.cloned.1.call-update) | async-done | bytes 4194320 | tf_op jit(solution)/shard_map/all_gather | solution.py:79
  145.2 4.0 convolution_convert_fusion
  150.0 4.7 all-to-all-start.4
  232.4 8.8 %pad.105 = f32[4,16,16]{0,2,1:T(8,128)} pad(f32[2,16,16]{0,2,1:T(8,128)} %pad_add_fusion, f32[]{:T(128)} %constant.10.clone.1), padding=1_0_1x0_0_0x0_0_0 | pad | bytes 6148 | tf_op jit(solution)/shard_map/pad | solution.py:36
  242.9 8.8 %pad.104 = f32[4,16,16]{0,2,1:T(8,128)} pad(f32[2,16,16]{0,2,1:T(8,128)} %pad_maximum_fusion.6, f32[]{:T(128)} %constant.10.clone.1), padding=0_1_1x0_0_0x0_0_0 | pad | bytes 6148 | tf_op jit(solution)/shard_map/pad | solution.py:36
  251.7 8.8 %pad.91 = f32[4,16,16]{0,2,1:T(8,128)} pad(f32[2,16,16]{0,2,1:T(8,128)} %pad_add_fusion.1, f32[]{:T(128)} %constant.10.clone.1), padding=1_0_1x0_0_0x0_0_0 | pad | bytes 6148 | tf_op jit(solution)/shard_map/pad | solution.py:36
  262.3 8.8 %pad.90 = f32[4,16,16]{0,2,1:T(8,128)} pad(f32[2,16,16]{0,2,1:T(8,128)} %pad_maximum_fusion, f32[]{:T(128)} %constant.10.clone.1), padding=0_1_1x0_0_0x0_0_0 | pad | bytes 6148 | tf_op jit(solution)/shard_map/pad | solution.py:36
  278.0 8.9 %pad.106 = f32[8,16,16]{0,2,1:T(8,128)} pad(f32[4,16,16]{0,2,1:T(8,128)} %pad_maximum_fusion.7, f32[]{:T(128)} %constant.10.clone.1), padding=0_1_1x0_0_0x0_0_0 | pad | bytes 12292 | tf_op jit(solution)/shard_map/pad | solution.py:36
  286.9 8.8 %pad.107 = f32[8,16,16]{0,2,1:T(8,128)} pad(f32[4,16,16]{0,2,1:T(8,128)} %add.248, f32[]{:T(128)} %constant.10.clone.1), padding=1_0_1x0_0_0x0_0_0 | pad | bytes 12292 | tf_op jit(solution)/shard_map/pad | solution.py:36
  297.3 8.9 %pad.109 = f32[16,16,16]{0,2,1:T(8,128)} pad(f32[8,16,16]{0,2,1:T(8,128)} %add.250, f32[]{:T(128)} %constant.10.clone.1), padding=1_0_1x0_0_0x0_0_0 | pad | bytes 24580 | tf_op jit(solution)/shard_map/pad | solution.py:36
  306.2 8.8 %pad.93 = f32[8,16,16]{0,2,1:T(8,128)} pad(f32[4,16,16]{0,2,1:T(8,128)} %add.225, f32[]{:T(128)} %constant.10.clone.1), padding=1_0_1x0_0_0x0_0_0 | pad | bytes 12292 | tf_op jit(solution)/shard_map/pad | solution.py:36
  316.7 6.2 pad.92
  327.9 6.3 pad.95
  335.9 6.3 pad.94
  348.0 6.5 pad.111
  356.7 6.5 pad.97
  364.8 6.5 pad.96
  376.0 6.8 pad.99
  395.8 43.1 %while.12 = (s32[]{:T(128)}, f32[16,16]{1,0:T(8,128)}, f32[16,16]{1,0:T(8,128)}, f32[128,32,16]{0,1,2:T(8,128)S(1)}, f32[128,32,16]{0,1,2:T(8,128)S(1)}, /*index=5*/s32[]{:T(128)}, s32[]{:T(128)}) while((s32[]{:T(128)}, f32[16,16]{1,0:T(8,128)}, f32[16,16]{1,0:T(8,128)}, f32[128,32,16]{0,1,2:T(8,128)S(1)}, ...), condition=%wide.region_5.6_spmd.clone.clone, body=%wide.region_3.5_spmd.clone.clone.sunk | while | flops 25431040 | bytes 533085 | solution.py:68
  452.4 19.7 %all_to_all.122 = bf16[32,128,16]{1,2,0:T(8,128)(2,1)S(1)} all-to-all(bf16[32,128,16]{1,2,0:T(8,128)(2,1)S(1)} %get-tuple-element.142), channel_id=1, replica_groups=mesh['ctx'=32,'chan'=8] {'ctx'}, dimensions={0} | all-to-all | bytes 262144 | tf_op jit(solution)/shard_map/all_to_all | solution.py:101
  472.2 4.3 fusion.79
  476.8 4.5 fusion.80
  500.0 10.0 %all-to-all-done.5 = bf16[32,128,16]{1,2,0:T(8,128)(2,1)S(1)} async-done(((bf16[32,128,16]{1,2,0:T(8,128)(2,1)}), bf16[32,128,16]{1,2,0:T(8,128)(2,1)S(1)}, u32[]{:S(2)}, u32[]{:S(2)}) %all-to-all-start.5) | async-done | bytes 131104 | tf_op jit(solution)/shard_map/all_to_all | solution.py:128
  515.2 42.7 %all_gather.14 = f32[512,16]{1,0:T(8,128)S(1)} all-gather(f32[16,16]{1,0:T(8,128)S(1)} %copy-done.17), channel_id=1, replica_groups=mesh['ctx'=32,'chan'=8] {'ctx'}, dimensions={0}, use_global_device_ids=true | all-gather | bytes 33792 | tf_op jit(solution)/shard_map/all_gather | solution.py:135
  557.8 5.0 all-to-all-start.7
  563.7 70.9 %all-reduce.30 = f32[512]{0:T(512)S(1)} all-reduce(f32[512]{0:T(512)S(1)} %dynamic-update-slice), channel_id=1, replica_groups=mesh['ctx'=32,'chan'=8] {'ctx'}, use_global_device_ids=true, to_apply=%add.30 | all-reduce | flops 512 | bytes 4096
  639.1 50.1 %reduce-scatter.5.cloned.1.call-done = f32[512,128]{1,0:T(8,128)} async-done(((f32[512,4096]{1,0:T(8,128)}), f32[512,128]{1,0:T(8,128)}) %reduce-scatter.5.cloned.1.call-update) | async-done | bytes 262160 | tf_op jit(solution)/shard_map/reduce_scatter | solution.py:113
  (264 shorter events, 227.8 us)
Async XLA Ops:
  7.2 47.8 %all-gather.5.cloned.1.call-start = ((), (), s32[]{:S(2)}) async-start(), calls=%async_computation.12 | async-start | bytes 1179648 | tf_op jit(solution)/shard_map/all_gather | solution.py:78
  7.9 137.3 %all-gather.3.cloned.1.call-start = ((), (), s32[]{:S(2)}) async-start(), calls=%async_computation.10 | async-start | bytes 4325376 | tf_op jit(solution)/shard_map/all_gather | solution.py:79
  10.3 22.1 %all-to-all-start.2 = ((bf16[128,32,16]{0,2,1:T(8,128)(2,1)}), bf16[128,32,16]{0,2,1:T(8,128)(2,1)S(1)}, u32[]{:S(2)}, u32[]{:S(2)}) async-start(bf16[128,32,16]{0,2,1:T(8,128)(2,1)} %bitcast.3), calls=%async_computation.2 | async-start | bytes 262144 | tf_op jit(solution)/shard_map/all_to_all | solution.py:82
  22.4 13.8 %copy-start.16 = (f32[16,16]{0,1:T(8,128)}, f32[16,16]{0,1:T(8,128)S(1)}, u32[]{:S(2)}) copy-start(f32[16,16]{0,1:T(8,128)S(1)} %get-tuple-element.190) | copy-start | bytes 3076
  24.2 125.1 %copy-start.15 = (f32[16,16]{1,0:T(8,128)}, f32[16,16]{1,0:T(8,128)S(1)}, u32[]{:S(2)}) copy-start(f32[16,16]{1,0:T(8,128)S(1)} %copy.147) | copy-start | bytes 3076
  24.8 154.2 %copy-start.14 = (f32[16,16]{1,0:T(8,128)}, f32[16,16]{1,0:T(8,128)S(1)}, u32[]{:S(2)}) copy-start(f32[16,16]{1,0:T(8,128)S(1)} %get-tuple-element.187) | copy-start | bytes 3076
  32.4 116.9 %copy-start.3 = (bf16[128,32,16]{0,2,1:T(8,128)(2,1)}, bf16[128,32,16]{0,2,1:T(8,128)(2,1)S(1)}, u32[]{:S(2)}) copy-start(bf16[128,32,16]{0,2,1:T(8,128)(2,1)S(1)} %all-to-all-done.2) | copy-start | bytes 393220
  32.4 14.6 %all-to-all-start.1 = ((bf16[128,32,16]{0,2,1:T(8,128)(2,1)}), bf16[128,32,16]{0,2,1:T(8,128)(2,1)S(1)}, u32[]{:S(2)}, u32[]{:S(2)}) async-start(bf16[128,32,16]{0,2,1:T(8,128)(2,1)} %bitcast.2), calls=%async_computation.1 | async-start | bytes 262144 | tf_op jit(solution)/shard_map/all_to_all | solution.py:81
  47.0 103.1 %copy-start.5 = (bf16[128,32,16]{0,2,1:T(8,128)(2,1)}, bf16[128,32,16]{0,2,1:T(8,128)(2,1)S(1)}, u32[]{:S(2)}) copy-start(bf16[128,32,16]{0,2,1:T(8,128)(2,1)S(1)} %all-to-all-done.1) | copy-start | bytes 393220
  47.0 103.1 %all-to-all-start = ((bf16[128,32,16]{0,2,1:T(8,128)(2,1)}), bf16[128,32,16]{0,2,1:T(8,128)(2,1)S(1)}, u32[]{:S(2)}, u32[]{:S(2)}) async-start(bf16[128,32,16]{0,2,1:T(8,128)(2,1)} %bitcast), calls=%async_computation | async-start | bytes 262144 | tf_op jit(solution)/shard_map/all_to_all | solution.py:83
  150.0 16.3 %copy-start.7 = (bf16[128,32,16]{0,2,1:T(8,128)(2,1)}, bf16[128,32,16]{0,2,1:T(8,128)(2,1)S(1)}, u32[]{:S(2)}) copy-start(bf16[128,32,16]{0,2,1:T(8,128)(2,1)S(1)} %all-to-all-done) | copy-start | bytes 393220
  150.0 15.5 %all-to-all-start.4 = ((bf16[128,32,16]{0,2,1:T(8,128)(2,1)}), bf16[128,32,16]{0,2,1:T(8,128)(2,1)S(1)}, u32[]{:S(2)}, u32[]{:S(2)}) async-start(bf16[128,32,16]{0,2,1:T(8,128)(2,1)} %bitcast.17), calls=%async_computation.5 | async-start | bytes 262144 | tf_op jit(solution)/shard_map/all_to_all | solution.py:115
  154.8 482.7 %reduce-scatter.3.cloned.1.call-start = ((), (), s32[]{:S(2)}) async-start(), calls=%async_computation.11 | async-start | bytes 2359296 | tf_op jit(solution)/shard_map/reduce_scatter | solution.py:103
  165.5 0.8 copy-start.9
  438.9 11.4 %copy-start.4 = (bf16[128,32,16]{0,2,1:T(8,128)(2,1)S(1)}, bf16[128,32,16]{0,2,1:T(8,128)(2,1)}, u32[]{:S(2)}) copy-start(bf16[128,32,16]{0,2,1:T(8,128)(2,1)} %copy-done.3) | copy-start | bytes 393220
  438.9 11.4 %copy-start.6 = (bf16[128,32,16]{0,2,1:T(8,128)(2,1)S(1)}, bf16[128,32,16]{0,2,1:T(8,128)(2,1)}, u32[]{:S(2)}) copy-start(bf16[128,32,16]{0,2,1:T(8,128)(2,1)} %copy-done.5) | copy-start | bytes 393220
  438.9 11.4 %copy-start.8 = (bf16[128,32,16]{0,2,1:T(8,128)(2,1)S(1)}, bf16[128,32,16]{0,2,1:T(8,128)(2,1)}, u32[]{:S(2)}) copy-start(bf16[128,32,16]{0,2,1:T(8,128)(2,1)} %copy-done.7) | copy-start | bytes 393220
  438.9 11.4 %copy-start.10 = (bf16[128,32,16]{0,2,1:T(8,128)(2,1)S(1)}, bf16[128,32,16]{0,2,1:T(8,128)(2,1)}, u32[]{:S(2)}) copy-start(bf16[128,32,16]{0,2,1:T(8,128)(2,1)} %copy-done.9) | copy-start | bytes 393220
  444.2 4.0 copy-start.12
  472.2 4.6 copy-start
  476.5 212.7 %reduce-scatter.5.cloned.1.call-start = ((), (), s32[]{:S(2)}) async-start(), calls=%async_computation.13 | async-start | bytes 8650752 | tf_op jit(solution)/shard_map/reduce_scatter | solution.py:113
  481.3 0.9 copy-start.11
  481.3 9.3 %copy-start.13 = (f32[16,16]{1,0:T(8,128)S(1)}, f32[16,16]{1,0:T(8,128)}, u32[]{:S(2)}) copy-start(f32[16,16]{1,0:T(8,128)} %copy-done.12) | copy-start | bytes 3076
  481.4 9.3 %copy-start.18 = (f32[128]{0:T(128)S(1)}, f32[128]{0:T(128)}, u32[]{:S(2)}) copy-start(f32[128]{0:T(128)} %iota_multiply_fusion.2) | copy-start | bytes 1540
  481.4 13.2 %copy-start.2 = (f32[32,2,8,128]{3,2,1,0:T(8,128)S(1)}, f32[32,2,8,128]{3,2,1,0:T(8,128)}, u32[]{:S(2)}) copy-start(f32[32,2,8,128]{3,2,1,0:T(8,128)} %copy-done.1) | copy-start | bytes 786436
  481.4 13.2 %copy-start.19 = (f32[16]{0:T(128)S(1)}, f32[16]{0:T(128)}, u32[]{:S(2)}) copy-start(f32[16]{0:T(128)} %dynamic_slice.17) | copy-start | bytes 196
  482.4 31.6 %copy-start.21 = (u32[256]{0:T(256)S(1)}, u32[256]{0:T(256)}, u32[]{:S(2)}) copy-start(u32[256]{0:T(256)} %constant.102) | copy-start | bytes 3076
  482.4 32.8 %copy-start.17 = (f32[16,16]{1,0:T(8,128)S(1)}, f32[16,16]{1,0:T(8,128)}, u32[]{:S(2)}) copy-start(f32[16,16]{1,0:T(8,128)} %get-tuple-element.156) | copy-start | bytes 3076
  488.9 74.7 %copy-start.20 = (f32[16]{0:T(128)S(1)}, f32[16]{0:T(128)}, u32[]{:S(2)}) copy-start(f32[16]{0:T(128)} %get-tuple-element.145) | copy-start | bytes 196
  495.5 14.6 %all-to-all-start.5 = ((bf16[32,128,16]{1,2,0:T(8,128)(2,1)}), bf16[32,128,16]{1,2,0:T(8,128)(2,1)S(1)}, u32[]{:S(2)}, u32[]{:S(2)}) async-start(bf16[32,128,16]{1,2,0:T(8,128)(2,1)} %bitcast.166), calls=%async_computation.6 | async-start | bytes 262144 | tf_op jit(solution)/shard_map/all_to_all | solution.py:128
  510.0 47.8 %all-to-all-start.6 = ((bf16[32,128,16]{1,2,0:T(8,128)(2,1)}), bf16[32,128,16]{1,2,0:T(8,128)(2,1)S(1)}, u32[]{:S(2)}, u32[]{:S(2)}) async-start(bf16[32,128,16]{1,2,0:T(8,128)(2,1)} %bitcast.165), calls=%async_computation.7 | async-start | bytes 262144 | tf_op jit(solution)/shard_map/all_to_all | solution.py:129
  557.8 78.9 %all-to-all-start.7 = ((bf16[32,128,16]{1,2,0:T(8,128)(2,1)}), bf16[32,128,16]{1,2,0:T(8,128)(2,1)S(1)}, u32[]{:S(2)}, u32[]{:S(2)}) async-start(bf16[32,128,16]{1,2,0:T(8,128)(2,1)} %get-tuple-element.141), calls=%async_computation.8 | async-start | bytes 262144 | tf_op jit(solution)/shard_map/all_to_all | solution.py:130
  (1 other events, 0.7 us)
Sparse Core Ops, SparseCore 0:
  9.8 45.1 all-gather.4
  57.6 87.5 all-gather.2
  476.7 52.5 reduce-scatter.2
  533.5 155.6 reduce-scatter.4
where the time goes:
time: 712 us; the launch traced here: 698 us
  local copies, waits for them, and re-layouts  242 us (34%)
  waiting for transfers between devices  166 us (23%)
  blocking collectives  133 us (19%)
  other arithmetic  64.7 us (9%)
  starting transfers between devices  38.7 us (5%)
  matrix products  37.5 us (5%)
  between operations  15.4 us (2%)
    pad x20, local copies, waits for them, and re-layouts, local_pass(): lax.associative_scan(combine_pair, (factors, block_ends), axis=0)[1]  125 us
    all_gather x1, waiting for transfers between devices, shards(): whole_weight = lax.all_gather(out_weight, 'ctx', axis=1, tiled=True)  90.2 us
    unnamed x1, blocking collectives  70.9 us
    slice x34, local copies, waits for them, and re-layouts, local_pass(): lax.associative_scan(combine_pair, (factors, block_ends), axis=0)[1]  53.1 us
    reduce_scatter x1, waiting for transfers between devices, shards(): lax.psum_scatter(weight_term, 'ctx', scatter_dimension=1, tiled=True)  50.1 us
    all_gather x1, blocking collectives, shards(): lax.all_gather(residue_terms, 'ctx', axis=0, tiled=True)  42.7 us
    dynamic_update_slice x16, local copies, waits for them, and re-layouts, mode_grad(): local_part = lax.map(one_mode, rates.T).T  20.8 us
    all_to_all x1, blocking collectives, shards(): lax.all_to_all(mixed_cols, 'ctx', split_axis=0, concat_axis=1, tiled=True)  19.7 us
  transfers between devices with their start and end apart: 11, of which 7 were waited for; matrix products, arithmetic and copies ran while one was open for 7% of the time, Pallas kernels for 0%

commit v1 on v0

v1 whole, which is shorter than its diff:
```python
import functools
import math

import jax
import jax.numpy as jnp
from jax import lax
from jax.experimental import pallas as pl
from jax.experimental.pallas import tpu as pltpu
from jax.sharding import PartitionSpec as P

MESH = pl.DeviceIdType.MESH
f32 = jnp.float32
bf16 = jnp.bfloat16

GROUP = 4
LANES = 128
SUBS = 8
MODES = 16
COPIES = 96


def one_minus_exp(x):
    series = jnp.ones_like(x)
    for n in range(9, 1, -1):
        series = 1.0 - x * (1.0 / n) * series
    return jnp.where(x < 0.5, x * series, 1.0 - jnp.exp(-x))


def kernel(
    zs, chans, length,
    q_ref, key_ref, gate_ref, cot_ref, w_ref, rate_ref, res_ref, skip_ref,
    final_ref, gq_ref, gk_ref, gg_ref, gw_ref, gres_ref, gskip_ref,
    gat_s, cotall, wall, xg, gateg, x_f, co_f, cg_f, pre_f, pre_b, e_all, b_all, l_all,
    mixed_all, og_own, og_send, og_recv, og_mid, fp, frecv, fin_g, fin_pos, gp, rsbuf,
    ggrp, ggpos, gates_g, gates_pos, tot_all,
    ss, rs,
):
    rows = q_ref.shape[0]
    span = rows * GROUP
    step_len = span // SUBS
    half = w_ref.shape[0] // 2
    scale = 1.0 / math.sqrt(length)

    i = lax.axis_index("ctx")
    j = lax.axis_index("chan")
    z = lax.div(i, GROUP)
    k = lax.rem(i, GROUP)
    k1 = k + 1 - 2 * lax.rem(k, 2)
    k2 = lax.rem(k + 2, GROUP)
    k3 = GROUP - 1 - k
    kp = {1: k1, 2: k2, 3: k3}

    def zmod(d):
        return lax.rem(z + d + zs, zs)

    def jmod(d):
        return lax.rem(j + d, chans)

    def g_peer(d):
        return {"ctx": z * GROUP + kp[d]}

    def z_peer(d):
        return {"ctx": zmod(d) * GROUP + k}

    def c_peer(d):
        return {"chan": jmod(d)}

    def lane(index):
        return pl.ds(pl.multiple_of(index * LANES, LANES), LANES)

    def row(index):
        return pl.ds(pl.multiple_of(index * rows, rows), rows)

    count = [0]
    started = []

    def remote(src, dst, peer):
        n = count[0]
        count[0] += 1
        copy = pltpu.make_async_remote_copy(
            src_ref=src, dst_ref=dst, send_sem=ss.at[n], recv_sem=rs.at[n],
            device_id=peer, device_id_type=MESH,
        )
        copy.start()
        started.append(copy)
        return copy

    barrier = pltpu.get_barrier_semaphore()
    peers = [g_peer(d) for d in (1, 2, 3)]
    peers += [z_peer(d) for d in range(1, zs)]
    peers += [c_peer(d) for d in range(1, chans)]
    for peer in peers:
        pl.semaphore_signal(barrier, inc=1, device_id=peer, device_id_type=MESH)

    own = pl.ds(pl.multiple_of(k * LANES, LANES), LANES)
    rate = jnp.transpose(rate_ref[own, :])
    inv_norm = jnp.sqrt(one_minus_exp(2.0 * rate) / one_minus_exp(2.0 * length * rate))
    gain = jnp.transpose(res_ref[own, :]) * inv_norm
    decay = jnp.exp(-rate)
    decay_sub = jnp.exp(-step_len * rate)
    decay_span = jnp.exp(-span * rate)
    skip = skip_ref[:, lane(k)]
    skip_b = jnp.broadcast_to(skip, (SUBS, LANES))
    sub = lax.broadcasted_iota(jnp.int32, (SUBS, LANES), 0)

    def spread(table, m):
        return jnp.broadcast_to(table[m : m + 1, :], (SUBS, LANES))

    gat_s[...] = (q_ref[...].astype(f32) * key_ref[...].astype(f32)).astype(bf16)
    pl.semaphore_wait(barrier, len(peers))

    chunk = (pl.ds(0, half), pl.ds(half, half))
    ring = {}
    lanes_for = ((1, 0, 4), (-1, 1, 4), (1, 1, 3), (-1, 0, 3))

    def weight_hop(h):
        for d, c, hops in lanes_for:
            if h > hops:
                continue
            block = lane(zmod(-d * (h - 1)))
            if h == 1:
                src = w_ref.at[chunk[c], :]
            else:
                ring[d, c, h - 1].wait_recv()
                src = wall.at[chunk[c], block]
            ring[d, c, h] = remote(src, wall.at[chunk[c], block], z_peer(d))

    cot_ex = [
        remote(cot_ref.at[:, lane(kp[d])], cotall.at[row(k), lane(j)], g_peer(d))
        for d in (2, 3, 1)
    ]
    weight_hop(1)
    sig_ex = []
    for d in (2, 3, 1):
        sig_ex.append(remote(gat_s.at[:, lane(kp[d])], xg.at[row(k), :], g_peer(d)))
        sig_ex.append(remote(gate_ref.at[:, lane(kp[d])], gateg.at[row(k), :], g_peer(d)))
    cotall[row(k), lane(j)] = cot_ref[:, lane(k)]
    xg[row(k), :] = gat_s[:, lane(k)]
    gateg[row(k), :] = gate_ref[:, lane(k)]
    wall[:, lane(z)] = w_ref[...]

    for copy in cot_ex:
        copy.wait_recv()
    cot_ag = [
        remote(cotall.at[:, lane(j)], cotall.at[:, lane(j)], c_peer(d))
        for d in range(1, chans)
    ]
    weight_hop(2)

    decays = [spread(decay, m) for m in range(MODES)]
    zero = jnp.zeros((SUBS, LANES), f32)

    def at_step(t):
        return pl.ds(t, SUBS, stride=step_len)

    def ends(src, backward):
        def body(s, state):
            t = step_len - 1 - s if backward else s
            value = src[at_step(t), :]
            return tuple(decays[m] * state[m] + value for m in range(MODES))

        return lax.fori_loop(0, step_len, body, (zero,) * MODES, unroll=4)

    def prefix(state, pre, backward, all_ref):
        for m in range(MODES):
            factor = spread(decay_sub, m)
            total = state[m]
            for shift in (1, 2, 4):
                moved = pltpu.roll(total, SUBS - shift if backward else shift, 0)
                keep = sub < SUBS - shift if backward else sub >= shift
                total = total + jnp.where(keep, factor * moved, 0.0)
                factor = factor * factor
            moved = pltpu.roll(total, SUBS - 1 if backward else 1, 0)
            pre[m] = jnp.where(sub < SUBS - 1 if backward else sub >= 1, moved, 0.0)
            edge = 0 if backward else SUBS - 1
            all_ref[z, m : m + 1, :] = total[edge : edge + 1, :]

    def carried(pre, all_ref, backward):
        carry = jnp.zeros((MODES, LANES), f32)
        for n in range(zs):
            other = zs - 1 - n if backward else n
            ahead = z < other if backward else z > other
            carry = jnp.where(ahead, decay_span * carry + all_ref[other], carry)
        steps = (SUBS - 1 - sub if backward else sub).astype(f32)
        return tuple(
            pre[m] + jnp.exp(-step_len * steps * spread(rate, m)) * spread(carry, m)
            for m in range(MODES)
        )

    def tree(terms):
        while len(terms) > 1:
            terms = [a + b for a, b in zip(terms[::2], terms[1::2])]
        return terms[0]

    gains = [spread(gain, m) for m in range(MODES)]

    def sweep(src, out, state, backward):
        def body(s, state):
            t = step_len - 1 - s if backward else s
            value = src[at_step(t), :]
            state = tuple(decays[m] * state[m] + value for m in range(MODES))
            out[at_step(t), :] = (
                tree([gains[m] * state[m] for m in range(MODES)]) + skip_b * value
            )
            return state

        lax.fori_loop(0, step_len, body, state, unroll=2)

    for copy in sig_ex:
        copy.wait_recv()
    x_f[...] = xg[...].astype(f32)
    prefix(ends(x_f, False), pre_f, False, e_all)
    e_ex = [
        remote(e_all.at[z], e_all.at[z], z_peer(d)) for d in (4, 3, 5, 2, 6, 1, 7)
    ]
    weight_hop(3)
    for copy in e_ex:
        copy.wait_recv()
    start_f = carried(pre_f, e_all, False)
    for m in range(MODES):
        pre_f[m] = start_f[m]
    sweep(x_f, co_f, start_f, False)
    mixed_all[:, lane(k)] = (gateg[...].astype(f32) * co_f[...]).astype(bf16)
    mix_2 = remote(mixed_all.at[:, lane(k)], mixed_all.at[:, lane(k)], g_peer(2))
    mix_1 = remote(mixed_all.at[:, lane(k)], mixed_all.at[:, lane(k)], g_peer(1))
    weight_hop(4)
    mix_2.wait_recv()
    mix_3 = remote(mixed_all.at[:, lane(k2)], mixed_all.at[:, lane(k2)], g_peer(1))
    for copy in cot_ag:
        copy.wait_recv()
    for d, c, hops in lanes_for:
        ring[d, c, hops].wait_recv()

    def out_grad_part(index):
        return lax.dot_general(
            cotall[...], wall[own_rows(index), :], (((1,), (1,)), ((), ())),
            preferred_element_type=f32,
        )

    def own_rows(index):
        return pl.ds(pl.multiple_of(index * LANES, LANES), LANES)

    og_send[0] = out_grad_part(k3).astype(bf16)
    og_a = remote(og_send.at[0], og_recv.at[0], g_peer(1))
    og_send[1] = out_grad_part(k1).astype(bf16)
    og_b = remote(og_send.at[1], og_recv.at[1], g_peer(1))
    og_mid[...] = out_grad_part(k2)
    og_own[...] = out_grad_part(k)
    og_a.wait_recv()
    og_send[2] = (og_mid[...] + og_recv[0].astype(f32)).astype(bf16)
    og_c = remote(og_send.at[2], og_recv.at[2], g_peer(2))

    mix_1.wait_recv()
    mix_3.wait_recv()
    pairs = wall.shape[1] // (2 * LANES)
    wide = 2 * LANES
    for n in range(pairs):
        fp[:, n * wide : (n + 1) * wide] = jnp.dot(
            mixed_all[...], wall[:, n * wide : (n + 1) * wide], preferred_element_type=f32
        ).astype(bf16)
    fin_ex = [
        remote(fp.at[:, lane(jmod(d))], frecv.at[d - 1], c_peer(d)) for d in range(1, chans)
    ]

    for n in range(pairs):
        gp[:, n * wide : (n + 1) * wide] = lax.dot_general(
            mixed_all[...], cotall[:, n * wide : (n + 1) * wide], (((0,), (0,)), ((), ())),
            preferred_element_type=f32,
        ).astype(bf16)
    sums = {}
    slots = {}
    for d, c, hops in lanes_for:
        for h in range(1, hops + 1):
            slots[d, c, h] = len(slots)

    def weight_sum_hop(h):
        for d, c, hops in lanes_for:
            if h > hops:
                continue
            block = lane(zmod(d * (hops - h + 1)))
            if h == 1:
                src = gp.at[chunk[c], block]
            else:
                sums[d, c, h - 1].wait_recv()
                slot = slots[d, c, h - 1]
                rsbuf[slot] = (
                    rsbuf[slot].astype(f32) + gp[chunk[c], block].astype(f32)
                ).astype(bf16)
                src = rsbuf.at[slot]
            sums[d, c, h] = remote(src, rsbuf.at[slots[d, c, h]], z_peer(d))

    weight_sum_hop(1)

    og_b.wait_recv()
    og_c.wait_recv()
    og = (og_own[...] + og_recv[1].astype(f32) + og_recv[2].astype(f32)).astype(bf16).astype(f32)
    cg_f[...] = og * gateg[...].astype(f32)
    gates_g[...] = (og * co_f[...]).astype(bf16)
    gate_ex = [
        remote(gates_g.at[row(kp[d]), :], gates_pos.at[:, lane(k)], g_peer(d)) for d in (2, 3, 1)
    ]
    gates_pos[:, lane(k)] = gates_g[row(k), :]
    prefix(ends(cg_f, True), pre_b, True, b_all)
    b_ex = [
        remote(b_all.at[z], b_all.at[z], z_peer(d)) for d in (4, 3, 5, 2, 6, 1, 7)
    ]
    weight_sum_hop(2)

    def residue_body(s, carry):
        state, sums_m = carry
        value = x_f[at_step(s), :]
        grad = cg_f[at_step(s), :]
        state = tuple(decays[m] * state[m] + value for m in range(MODES))
        return state, tuple(sums_m[m] + grad * state[m] for m in range(MODES))

    _, mode_sums = lax.fori_loop(
        0, step_len, residue_body,
        (tuple(pre_f[m] for m in range(MODES)), (zero,) * MODES), unroll=2,
    )
    for m in range(MODES):
        l_all[z, m : m + 1, :] = jnp.sum(mode_sums[m], axis=0, keepdims=True)
    l_all[z, MODES : MODES + 8, :] = jnp.broadcast_to(
        jnp.sum(cg_f[...] * x_f[...], axis=0, keepdims=True), (8, LANES)
    )
    l_ex = [
        remote(l_all.at[z], l_all.at[z], z_peer(d)) for d in (4, 3, 5, 2, 6, 1, 7)
    ]

    for copy in b_ex:
        copy.wait_recv()
    sweep(cg_f, co_f, carried(pre_b, b_all, True), True)
    ggrp[...] = co_f[...].astype(bf16)
    gg_ex = [
        remote(ggrp.at[row(kp[d]), :], ggpos.at[:, lane(k)], g_peer(d)) for d in (2, 3, 1)
    ]
    ggpos[:, lane(k)] = ggrp[row(k), :]
    weight_sum_hop(3)

    for copy in l_ex:
        copy.wait_recv()
    total = l_all[0]
    for n in range(1, zs):
        total = total + l_all[n]
    tot_all[0:MODES, lane(k)] = total[0:MODES] * inv_norm * scale
    tot_all[MODES : MODES + 8, lane(k)] = total[MODES : MODES + 8] * scale
    tot_ex = [
        remote(tot_all.at[:, lane(k)], tot_all.at[:, lane(k)], g_peer(d)) for d in (2, 3, 1)
    ]
    weight_sum_hop(4)

    for copy in gg_ex:
        copy.wait_recv()
    spread_grad = ggpos[...].astype(f32)
    gq_ref[...] = (spread_grad * key_ref[...].astype(f32)).astype(bf16)
    gk_ref[...] = (spread_grad * q_ref[...].astype(f32)).astype(bf16)
    for copy in gate_ex:
        copy.wait_recv()
    gg_ref[...] = gates_pos[...]

    for copy in fin_ex:
        copy.wait_recv()
    fin = fp[:, lane(j)].astype(f32)
    for n in range(chans - 1):
        fin = fin + frecv[n].astype(f32)
    fin_g[...] = fin.astype(bf16)
    out_ex = [
        remote(fin_g.at[row(kp[d]), :], fin_pos.at[:, lane(k)], g_peer(d)) for d in (2, 3, 1)
    ]
    fin_pos[:, lane(k)] = fin_g[row(k), :]

    for c in (0, 1):
        part = gp[chunk[c], lane(z)].astype(f32)
        for d, other, hops in lanes_for:
            if other == c:
                sums[d, c, hops].wait_recv()
                part = part + rsbuf[slots[d, c, hops]].astype(f32)
        gw_ref[chunk[c], :] = (part * scale).astype(bf16)

    for copy in tot_ex:
        copy.wait_recv()
    for n in range(GROUP):
        gres_ref[n * LANES : (n + 1) * LANES, :] = jnp.transpose(
            tot_all[0:MODES, n * LANES : (n + 1) * LANES]
        )
    gskip_ref[...] = tot_all[MODES : MODES + 1, :]
    for copy in out_ex:
        copy.wait_recv()
    final_ref[...] = fin_pos[...]
    for copy in started:
        copy.wait_send()


def shards(mesh, *args):
    q, key_input, gate, cot, weight, rates, residues, skip = args
    zs, chans = mesh.shape["ctx"] // GROUP, mesh.shape["chan"]
    rows, width = q.shape
    depth = weight.shape[0]
    span = rows * GROUP
    length = rows * mesh.shape["ctx"]
    columns = zs * LANES
    vmem = pl.BlockSpec(memory_space=pltpu.VMEM)
    shape = jax.ShapeDtypeStruct
    outs = pl.pallas_call(
        functools.partial(kernel, zs, chans, length),
        out_shape=(
            shape((rows, width), bf16),
            shape((rows, width), bf16),
            shape((rows, width), bf16),
            shape((rows, width), bf16),
            shape((depth, LANES), bf16),
            shape((width, MODES), f32),
            shape((1, width), f32),
        ),
        in_specs=[vmem] * 8,
        out_specs=(vmem,) * 7,
        scratch_shapes=[
            pltpu.VMEM((rows, width), bf16),
            pltpu.VMEM((span, columns), bf16),
            pltpu.VMEM((depth, columns), bf16),
            pltpu.VMEM((span, LANES), bf16),
            pltpu.VMEM((span, LANES), bf16),
            pltpu.VMEM((span, LANES), f32),
            pltpu.VMEM((span, LANES), f32),
            pltpu.VMEM((span, LANES), f32),
            pltpu.VMEM((MODES, SUBS, LANES), f32),
            pltpu.VMEM((MODES, SUBS, LANES), f32),
            pltpu.VMEM((zs, MODES, LANES), f32),
            pltpu.VMEM((zs, MODES, LANES), f32),
            pltpu.VMEM((zs, MODES + 8, LANES), f32),
            pltpu.VMEM((span, width), bf16),
            pltpu.VMEM((span, LANES), f32),
            pltpu.VMEM((3, span, LANES), bf16),
            pltpu.VMEM((3, span, LANES), bf16),
            pltpu.VMEM((span, LANES), f32),
            pltpu.VMEM((span, columns), bf16),
            pltpu.VMEM((chans - 1, span, LANES), bf16),
            pltpu.VMEM((span, LANES), bf16),
            pltpu.VMEM((rows, width), bf16),
            pltpu.VMEM((depth, columns), bf16),
            pltpu.VMEM((14, depth // 2, LANES), bf16),
            pltpu.VMEM((span, LANES), bf16),
            pltpu.VMEM((rows, width), bf16),
            pltpu.VMEM((span, LANES), bf16),
            pltpu.VMEM((rows, width), bf16),
            pltpu.VMEM((MODES + 8, width), f32),
            pltpu.SemaphoreType.DMA((COPIES,)),
            pltpu.SemaphoreType.DMA((COPIES,)),
        ],
        compiler_params=pltpu.CompilerParams(
            collective_id=0, has_side_effects=True, vmem_limit_bytes=48 * 2**20
        ),
    )(q, key_input, gate, cot, weight, rates, residues, skip.reshape(1, -1))
    return (*outs[:6], outs[6].reshape(-1))


def solution(mesh):
    placed = (
        P("ctx", "chan"),
        P("ctx", "chan"),
        P("ctx", "chan"),
        P("ctx", "chan"),
        P("chan", "ctx"),
        P("chan", None),
        P("chan", None),
        P("chan"),
    )
    return jax.shard_map(
        functools.partial(shards, mesh),
        mesh=mesh,
        in_specs=placed,
        out_specs=(
            P("ctx", "chan"),
            P("ctx", "chan"),
            P("ctx", "chan"),
            P("ctx", "chan"),
            P("chan", "ctx"),
            P("chan", None),
            P("chan"),
        ),
        check_vma=False,
    )
```

time: 712 us -> 67.7 us (0.10)
  the two profiles are of different devices: /device:TPU:8 before, /device:TPU:1 now
where the time goes in v1:
time: 67.7 us; the launch traced here: 67.6 us
  Pallas kernels  59.5 us (88%)
  local copies, waits for them, and re-layouts  7.34 us (11%)
  between operations  0.73 us (1%)
    pallas_call x1, Pallas kernels, shards(): pl.pallas_call(functools.partial(kernel, zs, chans, length), out_shape=(s...  59.5 us
    unnamed x23, local copies, waits for them, and re-layouts  7.34 us

profile of v1, /device:TPU:1, one launch (start us, length us, event | category | flops | bytes accessed | tf_op | source)
XLA Modules:
  0.0 67.6 jit_solution(10286461671722981538)
XLA Ops:
  0.6 0.0 copy-start.6
  0.6 0.0 copy-start.2
  0.7 0.0 copy-start.3
  0.7 0.9 %copy.15.rate_ref = f32[512,16]{1,0:T(8,128)S(1)} copy(f32[512,16]{0,1:T(8,128)} %param.13) | data formatting | bytes 65536 | tf_op args[5]
  1.6 0.0 copy-done.6
  1.6 0.0 copy-start
  1.6 0.0 copy-start.1
  1.6 0.0 copy-start.5
  1.6 0.1 copy.16.res_ref
  1.8 0.0 copy-done.2
  1.8 0.0 copy-done.3
  1.8 0.7 %copy-done = bf16[128,512]{1,0:T(8,128)(2,1)S(1)} copy-done((bf16[128,512]{1,0:T(8,128)(2,1)S(1)}, bf16[128,512]{1,0:T(8,128)(2,1)}, u32[]{:S(2)}) %copy-start) | copy-done | bytes 131096
  2.5 0.1 copy-done.1
  2.6 0.0 copy-done.5
  2.6 0.0 copy-start.4
  2.6 0.9 %copy-done.4 = bf16[512,128]{1,0:T(8,128)(2,1)S(1)} copy-done((bf16[512,128]{1,0:T(8,128)(2,1)S(1)}, bf16[512,128]{1,0:T(8,128)(2,1)}, u32[]{:S(2)}) %copy-start.4) | copy-done | bytes 131096
  3.5 59.5 %shard_map.135 = (bf16[128,512]{1,0:T(8,128)(2,1)S(1)}, bf16[128,512]{1,0:T(8,128)(2,1)S(1)}, bf16[128,512]{1,0:T(8,128)(2,1)S(1)}, bf16[128,512]{1,0:T(8,128)(2...) custom-call(bf16[128,512]{1,0:T(8,128)(2,1)S(1)} %copy-done, ...), custom_call_target="tpu_custom_call" | custom-call | tf_op jit(solution)/shard_map/pallas_call | solution.py:403
  63.0 0.7 %copy.17 = f32[512,16]{0,1:T(8,128)} copy(f32[512,16]{1,0:T(8,128)S(1)} %get-tuple-element.26) | data formatting | bytes 65536
  63.7 0.7 copy.24
  64.4 0.7 copy.25
  65.0 0.7 copy.26
  65.7 0.7 copy.27
  66.4 0.7 copy.28
  67.0 0.6 copy.29
Async XLA Ops:
  0.6 1.0 %copy-start.6 = (f32[512,16]{0,1:T(8,128)S(1)}, f32[512,16]{0,1:T(8,128)}, u32[]{:S(2)}) copy-start(f32[512,16]{0,1:T(8,128)} %param.14) | copy-start | bytes 98308
  0.6 1.1 %copy-start.2 = (bf16[128,512]{1,0:T(8,128)(2,1)S(1)}, bf16[128,512]{1,0:T(8,128)(2,1)}, u32[]{:S(2)}) copy-start(bf16[128,512]{1,0:T(8,128)(2,1)} %gate_ref.1) | copy-start | bytes 393220
  0.7 1.1 %copy-start.3 = (bf16[128,512]{1,0:T(8,128)(2,1)S(1)}, bf16[128,512]{1,0:T(8,128)(2,1)}, u32[]{:S(2)}) copy-start(bf16[128,512]{1,0:T(8,128)(2,1)} %cot_ref.1) | copy-start | bytes 393220
  1.6 0.9 %copy-start = (bf16[128,512]{1,0:T(8,128)(2,1)S(1)}, bf16[128,512]{1,0:T(8,128)(2,1)}, u32[]{:S(2)}) copy-start(bf16[128,512]{1,0:T(8,128)(2,1)} %q_ref.1) | copy-start | bytes 393220
  1.6 1.0 %copy-start.1 = (bf16[128,512]{1,0:T(8,128)(2,1)S(1)}, bf16[128,512]{1,0:T(8,128)(2,1)}, u32[]{:S(2)}) copy-start(bf16[128,512]{1,0:T(8,128)(2,1)} %key_ref.1) | copy-start | bytes 393220
  1.6 1.0 %copy-start.5 = (f32[512]{0:T(512)S(1)}, f32[512]{0:T(512)}, u32[]{:S(2)}) copy-start(f32[512]{0:T(512)} %param.15) | copy-start | bytes 6148
  2.6 0.9 %copy-start.4 = (bf16[512,128]{1,0:T(8,128)(2,1)S(1)}, bf16[512,128]{1,0:T(8,128)(2,1)}, u32[]{:S(2)}) copy-start(bf16[512,128]{1,0:T(8,128)(2,1)} %w_ref.1) | copy-start | bytes 393220

commit v2 on v1

v2 whole, which is shorter than its diff:
```python
import functools
import math

import jax
import jax.numpy as jnp
from jax import lax
from jax.experimental import pallas as pl
from jax.experimental.pallas import tpu as pltpu
from jax.sharding import PartitionSpec as P

MESH = pl.DeviceIdType.MESH
f32 = jnp.float32
bf16 = jnp.bfloat16

GROUP = 4
PAIR = 2
LANES = 128
SUBS = 8
MODES = 16


def one_minus_exp(x):
    series = jnp.ones_like(x)
    for n in range(9, 1, -1):
        series = 1.0 - x * (1.0 / n) * series
    return jnp.where(x < 0.5, x * series, 1.0 - jnp.exp(-x))


def kernel(
    zs, chans, length,
    q_hbm, key_hbm, gate_hbm, cot_hbm, w_hbm, rate_hbm, res_hbm, skip_hbm,
    final_ref, gq_ref, gk_ref, gg_ref, gw_ref, gres_ref, gskip_ref,
    q_ref, key_ref, gate_ref, cot_ref, w_ref, rate_ref, res_ref, skip_ref,
    gat_s, cotall, wall, xg, gateg, x_f, co_f, cg_f, pre_f, pre_b, e_all, b_all, l_all,
    mixed_all, og_acc, og_send, og_recv, fp, frecv, fin_y, fin_pos, gp, rsbuf,
    ggrp, ggpos, gates_g, tot_all, sizes,
    recv_sems, send_sems, load_sems,
):
    rows = q_ref.shape[0]
    span = rows * GROUP
    step_len = span // SUBS
    half = w_ref.shape[0] // 2
    ys = chans // PAIR
    wide = PAIR * LANES
    scale = 1.0 / math.sqrt(length)

    loads = [
        pltpu.make_async_copy(src, dst, load_sems.at[n])
        for n, (src, dst) in enumerate((
            (cot_hbm, cot_ref), (w_hbm, w_ref), (q_hbm, q_ref), (key_hbm, key_ref),
            (gate_hbm, gate_ref), (rate_hbm, rate_ref), (res_hbm, res_ref), (skip_hbm, skip_ref),
        ))
    ]
    for copy in loads:
        copy.start()

    i = lax.axis_index("ctx")
    j = lax.axis_index("chan")
    z = lax.div(i, GROUP)
    k = lax.rem(i, GROUP)
    y = lax.div(j, PAIR)
    xl = lax.rem(j, PAIR)
    k1 = k + 1 - 2 * lax.rem(k, 2)
    k2 = lax.rem(k + 2, GROUP)
    k3 = GROUP - 1 - k
    kp = {0: k, 1: k1, 2: k2, 3: k3}
    xp = {0: xl, 1: PAIR - 1 - xl}

    def zmod(d):
        return lax.rem(z + d + zs, zs)

    def ymod(d):
        return lax.rem(y + d + ys, ys)

    def x_peer(dk, dx):
        return {"ctx": z * GROUP + kp[dk], "chan": y * PAIR + xp[dx]}

    def z_peer(d):
        return {"ctx": zmod(d) * GROUP + k, "chan": j}

    def y_peer(d):
        return {"ctx": i, "chan": ymod(d) * PAIR + xl}

    x_order = [(dk, dx) for dk in (2, 3, 1, 0) for dx in (1, 0) if dk or dx]
    g_order = (2, 3, 1)
    z_order = [zs // 2] + [d for n in range(zs // 2 - 1, 0, -1) for d in (n, -n)]

    def lane(index):
        return pl.ds(pl.multiple_of(index * LANES, LANES), LANES)

    def pair(index):
        return pl.ds(pl.multiple_of(index * wide, wide), wide)

    def row(index):
        return pl.ds(pl.multiple_of(index * rows, rows), rows)

    counts = [0, 0]
    sent = []

    class Batch:
        def __init__(self, lane_class):
            self.recv = recv_sems.at[counts[0]]
            counts[0] += 1
            self.out = lane_class
            self.units = 0

        def send(self, src, dst, peer, units):
            pltpu.make_async_remote_copy(
                src_ref=src, dst_ref=dst, send_sem=self.out.sem, recv_sem=self.recv,
                device_id=peer, device_id_type=MESH,
            ).start()
            self.units += units
            self.out.units += units

        def wait(self):
            part = sizes.at[pl.ds(0, self.units)]
            pltpu.make_async_copy(part, part, self.recv).wait()

    class Outgoing:
        def __init__(self):
            self.sem = send_sems.at[counts[1]]
            counts[1] += 1
            self.units = 0
            sent.append(self)

        def wait(self):
            part = sizes.at[pl.ds(0, self.units)]
            pltpu.make_async_copy(part, part, self.sem).wait()

    block_u = rows // 16
    out_x, out_y, out_z, out_zs, out_s = (Outgoing() for _ in range(5))

    barrier = pltpu.get_barrier_semaphore()
    peers = [x_peer(*d) for d in x_order]
    peers += [z_peer(d) for d in z_order]
    peers += [y_peer(d) for d in range(1, ys)]
    for peer in peers:
        pl.semaphore_signal(barrier, inc=1, device_id=peer, device_id_type=MESH)

    for copy in loads:
        copy.wait()
    rate = rate_ref[:, lane(k)]
    inv_norm = jnp.sqrt(one_minus_exp(2.0 * rate) / one_minus_exp(2.0 * length * rate))
    gain = res_ref[:, lane(k)] * inv_norm
    decay = jnp.exp(-rate)
    decay_sub = jnp.exp(-step_len * rate)
    decay_span = jnp.exp(-span * rate)
    skip_b = jnp.broadcast_to(skip_ref[:, lane(k)], (SUBS, LANES))
    sub = lax.broadcasted_iota(jnp.int32, (SUBS, LANES), 0)

    def spread(table, m):
        return jnp.broadcast_to(table[m : m + 1, :], (SUBS, LANES))

    gat_s[...] = (q_ref[...].astype(f32) * key_ref[...].astype(f32)).astype(bf16)
    pl.semaphore_wait(barrier, len(peers))

    chunk = (pl.ds(0, half), pl.ds(half, half))
    ways = {0: ((1, 0, zs // 2), (-1, 1, zs // 2)), 1: ((1, 1, zs // 2 - 1), (-1, 0, zs // 2 - 1))}
    ring = {}
    chunk_u = half // 16

    def weight_hop(h, long):
        if h > 1:
            ring[h - 1, long].wait()
        if h > ways[long][0][2]:
            return
        ring[h, long] = Batch(out_z)
        for d, c, hops in ways[long]:
            block = lane(zmod(-d * (h - 1)))
            src = w_ref.at[chunk[c], :] if h == 1 else wall.at[chunk[c], block]
            ring[h, long].send(src, wall.at[chunk[c], block], z_peer(d), chunk_u)

    cot_x = Batch(out_x)
    for dk, dx in x_order:
        cot_x.send(
            cot_ref.at[:, lane(kp[dk])], cotall.at[row(k), lane(j)], x_peer(dk, dx), block_u
        )
    weight_hop(1, 0)
    weight_hop(1, 1)
    signals = Batch(out_x)
    for d in g_order:
        signals.send(gat_s.at[:, lane(kp[d])], xg.at[row(k), :], x_peer(d, 0), block_u)
        signals.send(gate_ref.at[:, lane(kp[d])], gateg.at[row(k), :], x_peer(d, 0), block_u)
    cotall[row(k), lane(j)] = cot_ref[:, lane(k)]
    xg[row(k), :] = gat_s[:, lane(k)]
    gateg[row(k), :] = gate_ref[:, lane(k)]
    wall[:, lane(z)] = w_ref[...]

    weight_hop(2, 0)
    cot_x.wait()
    cot_near = Batch(out_y)
    for d in (1, -1):
        cot_near.send(cotall.at[:, pair(y)], cotall.at[:, pair(y)], y_peer(d), 8 * block_u)
    cot_far = Batch(out_y)
    cot_far.send(cotall.at[:, pair(y)], cotall.at[:, pair(y)], y_peer(2), 8 * block_u)
    weight_hop(2, 1)

    decays = [spread(decay, m) for m in range(MODES)]
    gains = [spread(gain, m) for m in range(MODES)]
    zero = jnp.zeros((SUBS, LANES), f32)

    def at_step(t):
        return pl.ds(t, SUBS, stride=step_len)

    def ends(src, backward):
        def body(s, state):
            t = step_len - 1 - s if backward else s
            value = src[at_step(t), :]
            return tuple(decays[m] * state[m] + value for m in range(MODES))

        return lax.fori_loop(0, step_len, body, (zero,) * MODES, unroll=4)

    def prefix(state, pre, backward, all_ref):
        for m in range(MODES):
            factor = spread(decay_sub, m)
            total = state[m]
            for shift in (1, 2, 4):
                moved = pltpu.roll(total, SUBS - shift if backward else shift, 0)
                keep = sub < SUBS - shift if backward else sub >= shift
                total = total + jnp.where(keep, factor * moved, 0.0)
                factor = factor * factor
            moved = pltpu.roll(total, SUBS - 1 if backward else 1, 0)
            pre[m] = jnp.where(sub < SUBS - 1 if backward else sub >= 1, moved, 0.0)
            edge = 0 if backward else SUBS - 1
            all_ref[z, m : m + 1, :] = total[edge : edge + 1, :]

    def carried(pre, all_ref, backward):
        carry = jnp.zeros((MODES, LANES), f32)
        for n in range(zs):
            other = zs - 1 - n if backward else n
            ahead = z < other if backward else z > other
            carry = jnp.where(ahead, decay_span * carry + all_ref[other], carry)
        steps = (SUBS - 1 - sub if backward else sub).astype(f32)
        return tuple(
            pre[m] + jnp.exp(-step_len * steps * spread(rate, m)) * spread(carry, m)
            for m in range(MODES)
        )

    def tree(terms):
        while len(terms) > 1:
            terms = [a + b for a, b in zip(terms[::2], terms[1::2])]
        return terms[0]

    def sweep(src, out, state, backward):
        def body(s, state):
            t = step_len - 1 - s if backward else s
            value = src[at_step(t), :]
            state = tuple(decays[m] * state[m] + value for m in range(MODES))
            out[at_step(t), :] = (
                tree([gains[m] * state[m] for m in range(MODES)]) + skip_b * value
            )
            return state

        lax.fori_loop(0, step_len, body, state, unroll=2)

    def to_z(ref, units):
        batch = Batch(out_zs)
        for d in z_order:
            batch.send(ref.at[z], ref.at[z], z_peer(d), units)
        return batch

    signals.wait()
    x_f[...] = xg[...].astype(f32)
    prefix(ends(x_f, False), pre_f, False, e_all)
    e_batch = to_z(e_all, 2)
    weight_hop(3, 0)
    weight_hop(3, 1)
    e_batch.wait()
    start_f = carried(pre_f, e_all, False)
    for m in range(MODES):
        pre_f[m] = start_f[m]
    sweep(x_f, co_f, start_f, False)
    mixed_all[:, lane(k)] = (gateg[...].astype(f32) * co_f[...]).astype(bf16)
    mix_2 = Batch(out_x)
    mix_2.send(mixed_all.at[:, lane(k)], mixed_all.at[:, lane(k)], x_peer(2, 0), 4 * block_u)
    mix_1 = Batch(out_x)
    mix_1.send(mixed_all.at[:, lane(k)], mixed_all.at[:, lane(k)], x_peer(1, 0), 4 * block_u)
    weight_hop(4, 0)
    mix_2.wait()
    mix_1.send(mixed_all.at[:, lane(k2)], mixed_all.at[:, lane(k2)], x_peer(1, 0), 4 * block_u)
    weight_hop(4, 1)
    weight_hop(5, 0)
    mix_1.wait()

    for n in range(ys):
        cols = slice(n * wide, (n + 1) * wide)
        fp[:, cols] = jnp.dot(
            mixed_all[...], wall[:, cols], preferred_element_type=f32
        ).astype(bf16)
    fin_batch = Batch(out_y)
    for d in (1, -1, 2):
        fin_batch.send(
            fp.at[:, pair(ymod(d))], frecv.at[{1: 0, -1: 1, 2: 2}[d]], y_peer(d), 8 * block_u
        )

    def out_grad_part(d):
        return lax.dot_general(
            cotall[:, pair(ymod(d))], wall[:, pair(ymod(d))], (((1,), (1,)), ((), ())),
            preferred_element_type=f32,
        )

    cot_near.wait()
    og_acc[...] = out_grad_part(0)
    og_acc[...] += out_grad_part(1)
    og_acc[...] += out_grad_part(-1)
    cot_far.wait()
    og_acc[...] += out_grad_part(2)
    og_a = Batch(out_x)
    og_send[0] = og_acc[:, lane(k3)].astype(bf16)
    og_a.send(og_send.at[0], og_recv.at[0], x_peer(1, 0), 4 * block_u)
    og_b = Batch(out_x)
    og_send[1] = og_acc[:, lane(k1)].astype(bf16)
    og_b.send(og_send.at[1], og_recv.at[1], x_peer(1, 0), 4 * block_u)

    for n in range(ys):
        cols = slice(n * wide, (n + 1) * wide)
        gp[:, cols] = lax.dot_general(
            mixed_all[...], cotall[:, cols], (((0,), (0,)), ((), ())),
            preferred_element_type=f32,
        ).astype(bf16)
    sums = {}
    slots = {}
    for h in range(1, zs // 2 + 1):
        for long in (0, 1):
            for d, c, hops in ways[long]:
                if h <= hops:
                    slots[d, c, h] = len(slots)

    def weight_sum_hop(h, long):
        if h > 1:
            sums[h - 1, long].wait()
        if h > ways[long][0][2]:
            return
        sums[h, long] = Batch(out_s)
        for d, c, hops in ways[long]:
            block = lane(zmod(d * (hops - h + 1)))
            if h == 1:
                src = gp.at[chunk[c], block]
            else:
                slot = slots[d, c, h - 1]
                rsbuf[slot] = (
                    rsbuf[slot].astype(f32) + gp[chunk[c], block].astype(f32)
                ).astype(bf16)
                src = rsbuf.at[slot]
            sums[h, long].send(src, rsbuf.at[slots[d, c, h]], z_peer(d), chunk_u)

    weight_sum_hop(1, 0)
    weight_sum_hop(1, 1)
    og_a.wait()
    og_send[2] = (og_acc[:, lane(k2)] + og_recv[0].astype(f32)).astype(bf16)
    og_c = Batch(out_x)
    og_c.send(og_send.at[2], og_recv.at[2], x_peer(2, 0), 4 * block_u)
    weight_sum_hop(2, 0)

    og_b.wait()
    og_c.wait()
    og = og_acc[:, lane(k)] + og_recv[1].astype(f32) + og_recv[2].astype(f32)
    og = og.astype(bf16).astype(f32)
    cg_f[...] = og * gateg[...].astype(f32)
    prefix(ends(cg_f, True), pre_b, True, b_all)
    b_batch = to_z(b_all, 2)
    weight_sum_hop(2, 1)
    gates_g[...] = (og * co_f[...]).astype(bf16)
    gate_batch = Batch(out_x)
    for d in g_order:
        gate_batch.send(gates_g.at[row(kp[d]), :], gg_ref.at[:, lane(k)], x_peer(d, 0), block_u)
    gg_ref[:, lane(k)] = gates_g[row(k), :]

    def residue_body(s, carry):
        state, sums_m = carry
        value = x_f[at_step(s), :]
        grad = cg_f[at_step(s), :]
        state = tuple(decays[m] * state[m] + value for m in range(MODES))
        return state, tuple(sums_m[m] + grad * state[m] for m in range(MODES))

    _, mode_sums = lax.fori_loop(
        0, step_len, residue_body,
        (tuple(pre_f[m] for m in range(MODES)), (zero,) * MODES), unroll=2,
    )
    for m in range(MODES):
        l_all[z, m : m + 1, :] = jnp.sum(mode_sums[m], axis=0, keepdims=True)
    l_all[z, MODES : MODES + 8, :] = jnp.broadcast_to(
        jnp.sum(cg_f[...] * x_f[...], axis=0, keepdims=True), (8, LANES)
    )
    l_batch = to_z(l_all, 3)
    weight_sum_hop(3, 0)

    b_batch.wait()
    sweep(cg_f, co_f, carried(pre_b, b_all, True), True)
    ggrp[...] = co_f[...].astype(bf16)
    gg_batch = Batch(out_x)
    for d in g_order:
        gg_batch.send(ggrp.at[row(kp[d]), :], ggpos.at[:, lane(k)], x_peer(d, 0), block_u)
    ggpos[:, lane(k)] = ggrp[row(k), :]
    weight_sum_hop(3, 1)
    l_batch.wait()
    total = l_all[0]
    for n in range(1, zs):
        total = total + l_all[n]
    tot_all[0:MODES, lane(k)] = total[0:MODES] * inv_norm * scale
    tot_all[MODES : MODES + 8, lane(k)] = total[MODES : MODES + 8] * scale
    tot_batch = Batch(out_zs)
    for d in g_order:
        tot_batch.send(tot_all.at[:, lane(k)], tot_all.at[:, lane(k)], x_peer(d, 0), 3)
    weight_sum_hop(4, 0)

    fin_batch.wait()
    fin = fp[:, pair(y)].astype(f32)
    for n in range(ys - 1):
        fin = fin + frecv[n].astype(f32)
    fin_y[...] = fin.astype(bf16)
    out_batch = Batch(out_x)
    for dk, dx in x_order:
        out_batch.send(
            fin_y.at[row(kp[dk]), lane(xp[dx])], fin_pos.at[xl, :, lane(k)],
            x_peer(dk, dx), block_u,
        )
    fin_pos[xl, :, lane(k)] = fin_y[row(k), lane(xl)]

    gg_batch.wait()
    spread_grad = ggpos[...].astype(f32)
    gq_ref[...] = (spread_grad * key_ref[...].astype(f32)).astype(bf16)
    gk_ref[...] = (spread_grad * q_ref[...].astype(f32)).astype(bf16)
    gate_batch.wait()

    weight_sum_hop(4, 1)
    weight_sum_hop(5, 0)
    for c in (0, 1):
        part = gp[chunk[c], lane(z)].astype(f32)
        for long in (0, 1):
            for d, other, hops in ways[long]:
                if other == c:
                    part = part + rsbuf[slots[d, c, hops]].astype(f32)
        gw_ref[chunk[c], :] = (part * scale).astype(bf16)

    tot_batch.wait()
    gres_ref[...] = tot_all[0:MODES, :]
    gskip_ref[...] = tot_all[MODES : MODES + 1, :]
    out_batch.wait()
    final_ref[...] = (fin_pos[0].astype(f32) + fin_pos[1].astype(f32)).astype(bf16)
    for out in sent:
        out.wait()


def store_kernel(*refs):
    count = len(refs) // 2
    for n in range(count):
        refs[count + n][...] = refs[n][...]


def shards(mesh, *args):
    q, key_input, gate, cot, weight, rates, residues, skip = args
    zs, chans = mesh.shape["ctx"] // GROUP, mesh.shape["chan"]
    rows, width = q.shape
    depth = weight.shape[0]
    span = rows * GROUP
    length = rows * mesh.shape["ctx"]
    columns = zs * LANES
    vmem = pl.BlockSpec(memory_space=pltpu.VMEM)
    hbm = pl.BlockSpec(memory_space=pltpu.HBM)
    anywhere = pl.BlockSpec(memory_space=pl.ANY)
    shape = jax.ShapeDtypeStruct
    out_shape = (
        shape((rows, width), bf16),
        shape((rows, width), bf16),
        shape((rows, width), bf16),
        shape((rows, width), bf16),
        shape((depth, LANES), bf16),
        shape((MODES, width), f32),
        shape((1, width), f32),
    )
    outs = pl.pallas_call(
        functools.partial(kernel, zs, chans, length),
        out_shape=out_shape,
        in_specs=[hbm] * 8,
        out_specs=(vmem,) * 7,
        scratch_shapes=[
            pltpu.VMEM((rows, width), bf16),
            pltpu.VMEM((rows, width), bf16),
            pltpu.VMEM((rows, width), bf16),
            pltpu.VMEM((rows, width), bf16),
            pltpu.VMEM((depth, LANES), bf16),
            pltpu.VMEM((MODES, width), f32),
            pltpu.VMEM((MODES, width), f32),
            pltpu.VMEM((1, width), f32),
            pltpu.VMEM((rows, width), bf16),
            pltpu.VMEM((span, columns), bf16),
            pltpu.VMEM((depth, columns), bf16),
            pltpu.VMEM((span, LANES), bf16),
            pltpu.VMEM((span, LANES), bf16),
            pltpu.VMEM((span, LANES), f32),
            pltpu.VMEM((span, LANES), f32),
            pltpu.VMEM((span, LANES), f32),
            pltpu.VMEM((MODES, SUBS, LANES), f32),
            pltpu.VMEM((MODES, SUBS, LANES), f32),
            pltpu.VMEM((zs, MODES, LANES), f32),
            pltpu.VMEM((zs, MODES, LANES), f32),
            pltpu.VMEM((zs, MODES + 8, LANES), f32),
            pltpu.VMEM((span, width), bf16),
            pltpu.VMEM((span, width), f32),
            pltpu.VMEM((3, span, LANES), bf16),
            pltpu.VMEM((3, span, LANES), bf16),
            pltpu.VMEM((span, columns), bf16),
            pltpu.VMEM((chans // PAIR - 1, span, PAIR * LANES), bf16),
            pltpu.VMEM((span, PAIR * LANES), bf16),
            pltpu.VMEM((PAIR, rows, width), bf16),
            pltpu.VMEM((depth, columns), bf16),
            pltpu.VMEM((2 * (zs - 1), depth // 2, LANES), bf16),
            pltpu.VMEM((span, LANES), bf16),
            pltpu.VMEM((rows, width), bf16),
            pltpu.VMEM((span, LANES), bf16),
            pltpu.VMEM((MODES + 8, width), f32),
            pltpu.VMEM((512, 16, LANES), bf16),
            pltpu.SemaphoreType.DMA((32,)),
            pltpu.SemaphoreType.DMA((5,)),
            pltpu.SemaphoreType.DMA((8,)),
        ],
        compiler_params=pltpu.CompilerParams(
            collective_id=0, has_side_effects=True, vmem_limit_bytes=65000 * 1024
        ),
    )(q, key_input, gate, cot, weight, rates.T, residues.T, skip.reshape(1, -1))
    outs = pl.pallas_call(
        store_kernel,
        out_shape=out_shape,
        in_specs=[vmem] * 7,
        out_specs=(vmem,) * 7,
        compiler_params=pltpu.CompilerParams(vmem_limit_bytes=65000 * 1024),
    )(*outs)
    return (*outs[:5], outs[5].T, outs[6].reshape(-1))


def solution(mesh):
    placed = (
        P("ctx", "chan"),
        P("ctx", "chan"),
        P("ctx", "chan"),
        P("ctx", "chan"),
        P("chan", "ctx"),
        P("chan", None),
        P("chan", None),
        P("chan"),
    )
    return jax.shard_map(
        functools.partial(shards, mesh),
        mesh=mesh,
        in_specs=placed,
        out_specs=(
            P("ctx", "chan"),
            P("ctx", "chan"),
            P("ctx", "chan"),
            P("ctx", "chan"),
            P("chan", "ctx"),
            P("chan", None),
            P("chan"),
        ),
        check_vma=False,
    )
```

time: 67.7 us -> 55.7 us (0.82)
  local copies, waits for them, and re-layouts: 7.34 us -> 0 us
  Pallas kernels: 59.5 us -> 54.9 us
    unnamed x23 -> x0, local copies, waits for them, and re-layouts: 7.34 us -> none
    pallas_call x1 -> x2, Pallas kernels: 59.5 us -> 54.9 us  [the longest x1 52.9 us: shards(): pl.pallas_call(functools.partial(kernel, zs, chans, length), out_shape=ou...]
where the time goes in v2:
time: 55.7 us; the launch traced here: 55.6 us
  Pallas kernels  54.9 us (99%)
  between operations  0.64 us (1%)
    pallas_call x1, Pallas kernels, shards(): pl.pallas_call(functools.partial(kernel, zs, chans, length), out_shape=ou...  52.9 us
    pallas_call x1, Pallas kernels, shards(): pl.pallas_call(store_kernel, out_shape=out_shape, in_specs=[vmem] * 7, ou...  2.04 us

profile of v2, /device:TPU:1, one launch (start us, length us, event | category | flops | bytes accessed | tf_op | source)
XLA Modules:
  0.0 55.6 jit_solution(10654019920743633921)
XLA Ops:
  0.6 52.9 %shard_map.135 = (bf16[128,512]{1,0:T(8,128)(2,1)}, bf16[128,512]{1,0:T(8,128)(2,1)}, bf16[128,512]{1,0:T(8,128)(2,1)}, bf16[128,512]{1,0:T(8,128)(2,1)}, bf16[5...) custom-call(bf16[128,512]{1,0:T(8,128)(2,1)} %q_hbm.1, bf16[128,512]{1,0:T(8,128)(2,1)} %key_hbm.1, ...), custom_call_target="tpu_custom_call" | custom-call | tf_op jit(solution)/shard_map/pallas_call | solution.py:472
  53.5 2.0 %shard_map.136 = (bf16[128,512]{1,0:T(8,128)(2,1)}, bf16[128,512]{1,0:T(8,128)(2,1)}, bf16[128,512]{1,0:T(8,128)(2,1)}, bf16[128,512]{1,0:T(8,128)(2,1)}, bf16[5...) custom-call(bf16[128,512]{1,0:T(8,128)(2,1)} %get-tuple-element.21.refs_0_, ...), custom_call_target="tpu_custom_call" | custom-call | tf_op jit(solution)/shard_map/pallas_call | solution.py:522

commit v3 on v2

--- a/solution.py
+++ b/solution.py
@@ -29,11 +29,12 @@
 def kernel(
     zs, chans, length,
     q_hbm, key_hbm, gate_hbm, cot_hbm, w_hbm, rate_hbm, res_hbm, skip_hbm,
-    final_ref, gq_ref, gk_ref, gg_ref, gw_ref, gres_ref, gskip_ref,
+    final_hbm, gq_hbm, gk_hbm, gg_hbm, gw_hbm, gres_hbm, gskip_hbm,
     q_ref, key_ref, gate_ref, cot_ref, w_ref, rate_ref, res_ref, skip_ref,
-    gat_s, cotall, wall, xg, gateg, x_f, co_f, cg_f, pre_f, pre_b, e_all, b_all, l_all,
+    gat_s, cotall, wall, xg, gateg, x_f, co_f, cg_f, pre_f, pre_b, e_all, b_all, ends_s, l_all,
     mixed_all, og_acc, og_send, og_recv, fp, frecv, fin_y, fin_pos, gp, rsbuf,
     ggrp, ggpos, gates_g, tot_all, sizes,
+    final_ref, gq_ref, gk_ref, gg_ref, gw_ref,
     recv_sems, send_sems, load_sems,
 ):
     rows = q_ref.shape[0]
@@ -43,16 +44,6 @@
     ys = chans // PAIR
     wide = PAIR * LANES
     scale = 1.0 / math.sqrt(length)
-
-    loads = [
-        pltpu.make_async_copy(src, dst, load_sems.at[n])
-        for n, (src, dst) in enumerate((
-            (cot_hbm, cot_ref), (w_hbm, w_ref), (q_hbm, q_ref), (key_hbm, key_ref),
-            (gate_hbm, gate_ref), (rate_hbm, rate_ref), (res_hbm, res_ref), (skip_hbm, skip_ref),
-        ))
-    ]
-    for copy in loads:
-        copy.start()
 
     i = lax.axis_index("ctx")
     j = lax.axis_index("chan")
@@ -95,7 +86,6 @@
         return pl.ds(pl.multiple_of(index * rows, rows), rows)
 
     counts = [0, 0]
-    sent = []
 
     class Batch:
         def __init__(self, lane_class):
@@ -121,14 +111,15 @@
             self.sem = send_sems.at[counts[1]]
             counts[1] += 1
             self.units = 0
-            sent.append(self)
 
         def wait(self):
             part = sizes.at[pl.ds(0, self.units)]
             pltpu.make_async_copy(part, part, self.sem).wait()
 
     block_u = rows // 16
-    out_x, out_y, out_z, out_zs, out_s = (Outgoing() for _ in range(5))
+    out_x, out_y, out_z, out_zs, out_s, first_z = (
+        Outgoing() for _ in range(6)
+    )
 
     barrier = pltpu.get_barrier_semaphore()
     peers = [x_peer(*d) for d in x_order]
@@ -136,6 +127,16 @@
     peers += [y_peer(d) for d in range(1, ys)]
     for peer in peers:
         pl.semaphore_signal(barrier, inc=1, device_id=peer, device_id_type=MESH)
+
+    loads = [
+        pltpu.make_async_copy(src, dst, load_sems.at[n])
+        for n, (src, dst) in enumerate((
+            (cot_hbm, cot_ref), (w_hbm, w_ref), (q_hbm, q_ref), (key_hbm, key_ref),
+            (gate_hbm, gate_ref), (rate_hbm, rate_ref), (res_hbm, res_ref), (skip_hbm, skip_ref),
+        ))
+    ]
+    for copy in loads:
+        copy.start()
 
     for copy in loads:
         copy.wait()
@@ -164,36 +165,29 @@
             ring[h - 1, long].wait()
         if h > ways[long][0][2]:
             return
-        ring[h, long] = Batch(out_z)
+        ring[h, long] = Batch(first_z if (h, long) == (1, 0) else out_z)
         for d, c, hops in ways[long]:
             block = lane(zmod(-d * (h - 1)))
             src = w_ref.at[chunk[c], :] if h == 1 else wall.at[chunk[c], block]
             ring[h, long].send(src, wall.at[chunk[c], block], z_peer(d), chunk_u)
 
-    cot_x = Batch(out_x)
-    for dk, dx in x_order:
-        cot_x.send(
-            cot_ref.at[:, lane(kp[dk])], cotall.at[row(k), lane(j)], x_peer(dk, dx), block_u
-        )
-    weight_hop(1, 0)
-    weight_hop(1, 1)
+    y_order = (2, 1, -1)
     signals = Batch(out_x)
     for d in g_order:
         signals.send(gat_s.at[:, lane(kp[d])], xg.at[row(k), :], x_peer(d, 0), block_u)
-        signals.send(gate_ref.at[:, lane(kp[d])], gateg.at[row(k), :], x_peer(d, 0), block_u)
+    cot_a = Batch(out_x)
+    for d in g_order:
+        cot_a.send(
+            cot_ref.at[:, lane(kp[d])], cotall.at[row(k), lane(j)], x_peer(d, 0), block_u
+        )
+    cot_y = [Batch(out_y) for _ in range(3)]
+    for d in y_order:
+        cot_y[0].send(cot_ref.at[:, lane(k)], cotall.at[row(k), lane(j)], y_peer(d), block_u)
+    weight_hop(1, 0)
     cotall[row(k), lane(j)] = cot_ref[:, lane(k)]
     xg[row(k), :] = gat_s[:, lane(k)]
     gateg[row(k), :] = gate_ref[:, lane(k)]
     wall[:, lane(z)] = w_ref[...]
-
-    weight_hop(2, 0)
-    cot_x.wait()
-    cot_near = Batch(out_y)
-    for d in (1, -1):
-        cot_near.send(cotall.at[:, pair(y)], cotall.at[:, pair(y)], y_peer(d), 8 * block_u)
-    cot_far = Batch(out_y)
-    cot_far.send(cotall.at[:, pair(y)], cotall.at[:, pair(y)], y_peer(2), 8 * block_u)
-    weight_hop(2, 1)
 
     decays = [spread(decay, m) for m in range(MODES)]
     gains = [spread(gain, m) for m in range(MODES)]
@@ -222,14 +216,15 @@
             moved = pltpu.roll(total, SUBS - 1 if backward else 1, 0)
             pre[m] = jnp.where(sub < SUBS - 1 if backward else sub >= 1, moved, 0.0)
             edge = 0 if backward else SUBS - 1
-            all_ref[z, m : m + 1, :] = total[edge : edge + 1, :]
+            ends_s[m : m + 1, :] = total[edge : edge + 1, :]
+        all_ref[z] = ends_s[...].astype(bf16)
 
     def carried(pre, all_ref, backward):
         carry = jnp.zeros((MODES, LANES), f32)
         for n in range(zs):
             other = zs - 1 - n if backward else n
             ahead = z < other if backward else z > other
-            carry = jnp.where(ahead, decay_span * carry + all_ref[other], carry)
+            carry = jnp.where(ahead, decay_span * carry + all_ref[other].astype(f32), carry)
         steps = (SUBS - 1 - sub if backward else sub).astype(f32)
         return tuple(
             pre[m] + jnp.exp(-step_len * steps * spread(rate, m)) * spread(carry, m)
@@ -251,7 +246,7 @@
             )
             return state
 
-        lax.fori_loop(0, step_len, body, state, unroll=2)
+        lax.fori_loop(0, step_len, body, state, unroll=4)
 
     def to_z(ref, units):
         batch = Batch(out_zs)
@@ -259,10 +254,31 @@
             batch.send(ref.at[z], ref.at[z], z_peer(d), units)
         return batch
 
+    first_z.wait()
+    weight_hop(1, 1)
+    cot_b = Batch(out_x)
+    for dk in (1, 3, 2, 0):
+        cot_b.send(
+            cot_ref.at[:, lane(kp[dk])], cotall.at[row(k), lane(j)], x_peer(dk, 1), block_u
+        )
+    weight_hop(2, 0)
+    gates_in = Batch(out_x)
+    for d in g_order:
+        gates_in.send(gate_ref.at[:, lane(kp[d])], gateg.at[row(k), :], x_peer(d, 0), block_u)
+    cot_a.wait()
+    for dy in y_order:
+        for d in (1, 2, 3):
+            piece = (row(kp[d]), lane(j))
+            cot_y[1].send(cotall.at[piece], cotall.at[piece], y_peer(dy), block_u)
     signals.wait()
+    weight_hop(2, 1)
     x_f[...] = xg[...].astype(f32)
     prefix(ends(x_f, False), pre_f, False, e_all)
-    e_batch = to_z(e_all, 2)
+    e_batch = to_z(e_all, 1)
+    cot_b.wait()
+    other = (slice(None), lane(y * PAIR + xp[1]))
+    for dy in y_order:
+        cot_y[2].send(cotall.at[other], cotall.at[other], y_peer(dy), 4 * block_u)
     weight_hop(3, 0)
     weight_hop(3, 1)
     e_batch.wait()
@@ -270,6 +286,7 @@
     for m in range(MODES):
         pre_f[m] = start_f[m]
     sweep(x_f, co_f, start_f, False)
+    gates_in.wait()
     mixed_all[:, lane(k)] = (gateg[...].astype(f32) * co_f[...]).astype(bf16)
     mix_2 = Batch(out_x)
     mix_2.send(mixed_all.at[:, lane(k)], mixed_all.at[:, lane(k)], x_peer(2, 0), 4 * block_u)
@@ -280,6 +297,25 @@
     mix_1.send(mixed_all.at[:, lane(k2)], mixed_all.at[:, lane(k2)], x_peer(1, 0), 4 * block_u)
     weight_hop(4, 1)
     weight_hop(5, 0)
+    def out_grad_part(d):
+        return lax.dot_general(
+            cotall[:, pair(ymod(d))], wall[:, pair(ymod(d))], (((1,), (1,)), ((), ())),
+            preferred_element_type=f32,
+        )
+
+    og_acc[...] = out_grad_part(0)
+    for batch in cot_y:
+        batch.wait()
+    og_acc[...] += out_grad_part(1)
+    og_acc[...] += out_grad_part(-1)
+    og_acc[...] += out_grad_part(2)
+    og_a = Batch(out_x)
+    og_send[0] = og_acc[:, lane(k3)].astype(bf16)
+    og_a.send(og_send.at[0], og_recv.at[0], x_peer(1, 0), 4 * block_u)
+    og_b = Batch(out_x)
+    og_send[1] = og_acc[:, lane(k1)].astype(bf16)
+    og_b.send(og_send.at[1], og_recv.at[1], x_peer(1, 0), 4 * block_u)
+
     mix_1.wait()
 
     for n in range(ys):
@@ -293,25 +329,10 @@
             fp.at[:, pair(ymod(d))], frecv.at[{1: 0, -1: 1, 2: 2}[d]], y_peer(d), 8 * block_u
         )
 
-    def out_grad_part(d):
-        return lax.dot_general(
-            cotall[:, pair(ymod(d))], wall[:, pair(ymod(d))], (((1,), (1,)), ((), ())),
-            preferred_element_type=f32,
-        )
-
-    cot_near.wait()
-    og_acc[...] = out_grad_part(0)
-    og_acc[...] += out_grad_part(1)
-    og_acc[...] += out_grad_part(-1)
-    cot_far.wait()
-    og_acc[...] += out_grad_part(2)
-    og_a = Batch(out_x)
-    og_send[0] = og_acc[:, lane(k3)].astype(bf16)
-    og_a.send(og_send.at[0], og_recv.at[0], x_peer(1, 0), 4 * block_u)
-    og_b = Batch(out_x)
-    og_send[1] = og_acc[:, lane(k1)].astype(bf16)
-    og_b.send(og_send.at[1], og_recv.at[1], x_peer(1, 0), 4 * block_u)
-
+    og_a.wait()
+    og_send[2] = (og_acc[:, lane(k2)] + og_recv[0].astype(f32)).astype(bf16)
+    og_c = Batch(out_x)
+    og_c.send(og_send.at[2], og_recv.at[2], x_peer(2, 0), 4 * block_u)
     for n in range(ys):
         cols = slice(n * wide, (n + 1) * wide)
         gp[:, cols] = lax.dot_general(
@@ -346,20 +367,16 @@
 
     weight_sum_hop(1, 0)
     weight_sum_hop(1, 1)
-    og_a.wait()
-    og_send[2] = (og_acc[:, lane(k2)] + og_recv[0].astype(f32)).astype(bf16)
-    og_c = Batch(out_x)
-    og_c.send(og_send.at[2], og_recv.at[2], x_peer(2, 0), 4 * block_u)
     weight_sum_hop(2, 0)
 
+    weight_sum_hop(2, 1)
     og_b.wait()
     og_c.wait()
     og = og_acc[:, lane(k)] + og_recv[1].astype(f32) + og_recv[2].astype(f32)
     og = og.astype(bf16).astype(f32)
     cg_f[...] = og * gateg[...].astype(f32)
     prefix(ends(cg_f, True), pre_b, True, b_all)
-    b_batch = to_z(b_all, 2)
-    weight_sum_hop(2, 1)
+    b_batch = to_z(b_all, 1)
     gates_g[...] = (og * co_f[...]).astype(bf16)
     gate_batch = Batch(out_x)
     for d in g_order:
@@ -375,7 +392,7 @@
 
     _, mode_sums = lax.fori_loop(
         0, step_len, residue_body,
-        (tuple(pre_f[m] for m in range(MODES)), (zero,) * MODES), unroll=2,
+        (tuple(pre_f[m] for m in range(MODES)), (zero,) * MODES), unroll=4,
     )
     for m in range(MODES):
         l_all[z, m : m + 1, :] = jnp.sum(mode_sums[m], axis=0, keepdims=True)
@@ -385,6 +402,7 @@
     l_batch = to_z(l_all, 3)
     weight_sum_hop(3, 0)
 
+    weight_sum_hop(3, 1)
     b_batch.wait()
     sweep(cg_f, co_f, carried(pre_b, b_all, True), True)
     ggrp[...] = co_f[...].astype(bf16)
@@ -392,16 +410,6 @@
     for d in g_order:
         gg_batch.send(ggrp.at[row(kp[d]), :], ggpos.at[:, lane(k)], x_peer(d, 0), block_u)
     ggpos[:, lane(k)] = ggrp[row(k), :]
-    weight_sum_hop(3, 1)
-    l_batch.wait()
-    total = l_all[0]
-    for n in range(1, zs):
-        total = total + l_all[n]
-    tot_all[0:MODES, lane(k)] = total[0:MODES] * inv_norm * scale
-    tot_all[MODES : MODES + 8, lane(k)] = total[MODES : MODES + 8] * scale
-    tot_batch = Batch(out_zs)
-    for d in g_order:
-        tot_batch.send(tot_all.at[:, lane(k)], tot_all.at[:, lane(k)], x_peer(d, 0), 3)
     weight_sum_hop(4, 0)
 
     fin_batch.wait()
@@ -417,11 +425,30 @@
         )
     fin_pos[xl, :, lane(k)] = fin_y[row(k), lane(xl)]
 
+    l_batch.wait()
+    total = l_all[0]
+    for n in range(1, zs):
+        total = total + l_all[n]
+    tot_all[0:MODES, lane(k)] = total[0:MODES] * inv_norm * scale
+    tot_all[MODES : MODES + 8, lane(k)] = total[MODES : MODES + 8] * scale
+    tot_batch = Batch(out_zs)
+    for d in g_order:
+        tot_batch.send(tot_all.at[:, lane(k)], tot_all.at[:, lane(k)], x_peer(d, 0), 3)
+    writes = []
+
+    def write(n, src, dst):
+        copy = pltpu.make_async_copy(src, dst, load_sems.at[n])
+        copy.start()
+        writes.append(copy)
+
     gg_batch.wait()
     spread_grad = ggpos[...].astype(f32)
     gq_ref[...] = (spread_grad * key_ref[...].astype(f32)).astype(bf16)
     gk_ref[...] = (spread_grad * q_ref[...].astype(f32)).astype(bf16)
+    write(1, gq_ref, gq_hbm)
+    write(2, gk_ref, gk_hbm)
     gate_batch.wait()
+    write(3, gg_ref, gg_hbm)
 
     weight_sum_hop(4, 1)
     weight_sum_hop(5, 0)
@@ -432,20 +459,33 @@
                 if other == c:
                     part = part + rsbuf[slots[d, c, hops]].astype(f32)
         gw_ref[chunk[c], :] = (part * scale).astype(bf16)
+    write(4, gw_ref, gw_hbm)
 
     tot_batch.wait()
-    gres_ref[...] = tot_all[0:MODES, :]
-    gskip_ref[...] = tot_all[MODES : MODES + 1, :]
+    write(5, tot_all.at[pl.ds(0, MODES), :], gres_hbm)
+    write(6, tot_all.at[pl.ds(MODES, 1), :], gskip_hbm)
     out_batch.wait()
     final_ref[...] = (fin_pos[0].astype(f32) + fin_pos[1].astype(f32)).astype(bf16)
-    for out in sent:
+    write(0, final_ref, final_hbm)
+    for out in (out_x, out_y, out_z, out_zs, out_s):
         out.wait()
+    for copy in writes:
+        copy.wait()
 
 
 def store_kernel(*refs):
-    count = len(refs) // 2
-    for n in range(count):
-        refs[count + n][...] = refs[n][...]
+    count = (len(refs) - 2) // 3
+    srcs, dsts, bufs = refs[:count], refs[count : 2 * count], refs[2 * count : 3 * count]
+    in_sems, out_sems = refs[3 * count :]
+    reads = [pltpu.make_async_copy(srcs[n], bufs[n], in_sems.at[n]) for n in range(count)]
+    writes = [pltpu.make_async_copy(bufs[n], dsts[n], out_sems.at[n]) for n in range(count)]
+    for copy in reads:
+        copy.start()
+    for read, write in zip(reads, writes):
+        read.wait()
+        write.start()
+    for copy in writes:
+        copy.wait()
 
 
 def shards(mesh, *args):
@@ -456,9 +496,7 @@
     span = rows * GROUP
     length = rows * mesh.shape["ctx"]
     columns = zs * LANES
-    vmem = pl.BlockSpec(memory_space=pltpu.VMEM)
     hbm = pl.BlockSpec(memory_space=pltpu.HBM)
-    anywhere = pl.BlockSpec(memory_space=pl.ANY)
     shape = jax.ShapeDtypeStruct
     out_shape = (
         shape((rows, width), bf16),
@@ -473,7 +511,7 @@
         functools.partial(kernel, zs, chans, length),
         out_shape=out_shape,
         in_specs=[hbm] * 8,
-        out_specs=(vmem,) * 7,
+        out_specs=(hbm,) * 7,
         scratch_shapes=[
             pltpu.VMEM((rows, width), bf16),
             pltpu.VMEM((rows, width), bf16),
@@ -493,8 +531,9 @@
             pltpu.VMEM((span, LANES), f32),
             pltpu.VMEM((MODES, SUBS, LANES), f32),
             pltpu.VMEM((MODES, SUBS, LANES), f32),
-            pltpu.VMEM((zs, MODES, LANES), f32),
-            pltpu.VMEM((zs, MODES, LANES), f32),
+            pltpu.VMEM((zs, MODES, LANES), bf16),
+            pltpu.VMEM((zs, MODES, LANES), bf16),
+            pltpu.VMEM((MODES, LANES), f32),
             pltpu.VMEM((zs, MODES + 8, LANES), f32),
             pltpu.VMEM((span, width), bf16),
             pltpu.VMEM((span, width), f32),
@@ -511,8 +550,9 @@
             pltpu.VMEM((span, LANES), bf16),
             pltpu.VMEM((MODES + 8, width), f32),
             pltpu.VMEM((512, 16, LANES), bf16),
-            pltpu.SemaphoreType.DMA((32,)),
-            pltpu.SemaphoreType.DMA((5,)),
+            *[pltpu.VMEM(a.shape, a.dtype) for a in out_shape[:5]],
+            pltpu.SemaphoreType.DMA((36,)),
+            pltpu.SemaphoreType.DMA((6,)),
             pltpu.SemaphoreType.DMA((8,)),
         ],
         compiler_params=pltpu.CompilerParams(
@@ -522,8 +562,13 @@
     outs = pl.pallas_call(
         store_kernel,
         out_shape=out_shape,
-        in_specs=[vmem] * 7,
-        out_specs=(vmem,) * 7,
+        in_specs=[hbm] * 7,
+        out_specs=(hbm,) * 7,
+        scratch_shapes=[
+            *[pltpu.VMEM(a.shape, a.dtype) for a in out_shape],
+            pltpu.SemaphoreType.DMA((7,)),
+            pltpu.SemaphoreType.DMA((7,)),
+        ],
         compiler_params=pltpu.CompilerParams(vmem_limit_bytes=65000 * 1024),
     )(*outs)
     return (*outs[:5], outs[5].T, outs[6].reshape(-1))

time: 55.7 us -> 54.3 us (0.975)
  Pallas kernels: 54.9 us -> 53.5 us
    pallas_call x1, Pallas kernels: 52.9 us -> 51.6 us  [shards(): pl.pallas_call(functools.partial(kernel, zs, chans, length), out_shape=ou...]
where the time goes in v3:
time: 54.3 us; the launch traced here: 54.1 us
  Pallas kernels  53.5 us (99%)
  between operations  0.64 us (1%)
    pallas_call x1, Pallas kernels, shards(): pl.pallas_call(functools.partial(kernel, zs, chans, length), out_shape=ou...  51.6 us
    pallas_call x1, Pallas kernels, shards(): pl.pallas_call(store_kernel, out_shape=out_shape, in_specs=[hbm] * 7, out...  1.95 us

profile of v3, /device:TPU:1, one launch (start us, length us, event | category | flops | bytes accessed | tf_op | source)
XLA Modules:
  0.0 54.1 jit_solution(9765348848591580045)
XLA Ops:
  0.6 51.6 %shard_map.135 = (bf16[128,512]{1,0:T(8,128)(2,1)}, bf16[128,512]{1,0:T(8,128)(2,1)}, bf16[128,512]{1,0:T(8,128)(2,1)}, bf16[128,512]{1,0:T(8,128)(2,1)}, bf16[5...) custom-call(bf16[128,512]{1,0:T(8,128)(2,1)} %q_hbm.1, bf16[128,512]{1,0:T(8,128)(2,1)} %key_hbm.1, ...), custom_call_target="tpu_custom_call" | custom-call | tf_op jit(solution)/shard_map/pallas_call | solution.py:510
  52.2 1.9 %shard_map.136 = (bf16[128,512]{1,0:T(8,128)(2,1)}, bf16[128,512]{1,0:T(8,128)(2,1)}, bf16[128,512]{1,0:T(8,128)(2,1)}, bf16[128,512]{1,0:T(8,128)(2,1)}, bf16[5...) custom-call(bf16[128,512]{1,0:T(8,128)(2,1)} %get-tuple-element.21.refs_0_, ...), custom_call_target="tpu_custom_call" | custom-call | tf_op jit(solution)/shard_map/pallas_call | solution.py:562

commit v4 on v3

--- a/solution.py
+++ b/solution.py
@@ -17,6 +17,8 @@
 LANES = 128
 SUBS = 8
 MODES = 16
+RECEIVES = 38
+SENDS = 6
 
 
 def one_minus_exp(x):
@@ -31,7 +33,7 @@
     q_hbm, key_hbm, gate_hbm, cot_hbm, w_hbm, rate_hbm, res_hbm, skip_hbm,
     final_hbm, gq_hbm, gk_hbm, gg_hbm, gw_hbm, gres_hbm, gskip_hbm,
     q_ref, key_ref, gate_ref, cot_ref, w_ref, rate_ref, res_ref, skip_ref,
-    gat_s, cotall, wall, xg, gateg, x_f, co_f, cg_f, pre_f, pre_b, e_all, b_all, ends_s, l_all,
+    gat_s, two_ref, cotall, wall, xg, gateg, x_f, co_f, cg_f, pre_f, pre_b, e_all, b_all, ends_s, l_s, l_all,
     mixed_all, og_acc, og_send, og_recv, fp, frecv, fin_y, fin_pos, gp, rsbuf,
     ggrp, ggpos, gates_g, tot_all, sizes,
     final_ref, gq_ref, gk_ref, gg_ref, gw_ref,
@@ -138,8 +140,47 @@
     for copy in loads:
         copy.start()
 
+    pl.semaphore_wait(barrier, len(peers))
+
+    chunk = (pl.ds(0, half), pl.ds(half, half))
+    ways = {0: ((1, 0, zs // 2), (-1, 1, zs // 2)), 1: ((1, 1, zs // 2 - 1), (-1, 0, zs // 2 - 1))}
+    ring = {}
+    chunk_u = half // 16
+
+    def weight_hop(h, long):
+        if h > 1:
+            ring[h - 1, long].wait()
+        if h > ways[long][0][2]:
+            return
+        ring[h, long] = Batch(first_z if (h, long) == (1, 0) else out_z)
+        for d, c, hops in ways[long]:
+            block = lane(zmod(-d * (h - 1)))
+            src = w_hbm.at[chunk[c], :] if h == 1 else wall.at[chunk[c], block]
+            ring[h, long].send(src, wall.at[chunk[c], block], z_peer(d), chunk_u)
+
+    y_order = (2, 1, -1)
+    cot_y = [Batch(out_y) for _ in range(3)]
+    for d in (1, -1):
+        cot_y[0].send(cot_hbm.at[:, lane(k)], cotall.at[row(k), lane(j)], y_peer(d), block_u)
+    cot_two = Batch(out_y)
+    cot_two.send(cot_hbm, two_ref, y_peer(2), 4 * block_u)
+    weight_hop(1, 0)
     for copy in loads:
         copy.wait()
+    gat_s[...] = (q_ref[...].astype(f32) * key_ref[...].astype(f32)).astype(bf16)
+    signals = Batch(out_x)
+    for d in g_order:
+        signals.send(gat_s.at[:, lane(kp[d])], xg.at[row(k), :], x_peer(d, 0), block_u)
+    cot_a = Batch(out_x)
+    for d in g_order:
+        cot_a.send(
+            cot_hbm.at[:, lane(kp[d])], cotall.at[row(k), lane(j)], x_peer(d, 0), block_u
+        )
+    cotall[row(k), lane(j)] = cot_ref[:, lane(k)]
+    xg[row(k), :] = gat_s[:, lane(k)]
+    gateg[row(k), :] = gate_ref[:, lane(k)]
+    wall[:, lane(z)] = w_ref[...]
+
     rate = rate_ref[:, lane(k)]
     inv_norm = jnp.sqrt(one_minus_exp(2.0 * rate) / one_minus_exp(2.0 * length * rate))
     gain = res_ref[:, lane(k)] * inv_norm
@@ -151,43 +192,6 @@
 
     def spread(table, m):
         return jnp.broadcast_to(table[m : m + 1, :], (SUBS, LANES))
-
-    gat_s[...] = (q_ref[...].astype(f32) * key_ref[...].astype(f32)).astype(bf16)
-    pl.semaphore_wait(barrier, len(peers))
-
-    chunk = (pl.ds(0, half), pl.ds(half, half))
-    ways = {0: ((1, 0, zs // 2), (-1, 1, zs // 2)), 1: ((1, 1, zs // 2 - 1), (-1, 0, zs // 2 - 1))}
-    ring = {}
-    chunk_u = half // 16
-
-    def weight_hop(h, long):
-        if h > 1:
-            ring[h - 1, long].wait()
-        if h > ways[long][0][2]:
-            return
-        ring[h, long] = Batch(first_z if (h, long) == (1, 0) else out_z)
-        for d, c, hops in ways[long]:
-            block = lane(zmod(-d * (h - 1)))
-            src = w_ref.at[chunk[c], :] if h == 1 else wall.at[chunk[c], block]
-            ring[h, long].send(src, wall.at[chunk[c], block], z_peer(d), chunk_u)
-
-    y_order = (2, 1, -1)
-    signals = Batch(out_x)
-    for d in g_order:
-        signals.send(gat_s.at[:, lane(kp[d])], xg.at[row(k), :], x_peer(d, 0), block_u)
-    cot_a = Batch(out_x)
-    for d in g_order:
-        cot_a.send(
-            cot_ref.at[:, lane(kp[d])], cotall.at[row(k), lane(j)], x_peer(d, 0), block_u
-        )
-    cot_y = [Batch(out_y) for _ in range(3)]
-    for d in y_order:
-        cot_y[0].send(cot_ref.at[:, lane(k)], cotall.at[row(k), lane(j)], y_peer(d), block_u)
-    weight_hop(1, 0)
-    cotall[row(k), lane(j)] = cot_ref[:, lane(k)]
-    xg[row(k), :] = gat_s[:, lane(k)]
-    gateg[row(k), :] = gate_ref[:, lane(k)]
-    wall[:, lane(z)] = w_ref[...]
 
     decays = [spread(decay, m) for m in range(MODES)]
     gains = [spread(gain, m) for m in range(MODES)]
@@ -219,7 +223,7 @@
             ends_s[m : m + 1, :] = total[edge : edge + 1, :]
         all_ref[z] = ends_s[...].astype(bf16)
 
-    def carried(pre, all_ref, backward):
+    def carried(all_ref, backward):
         carry = jnp.zeros((MODES, LANES), f32)
         for n in range(zs):
             other = zs - 1 - n if backward else n
@@ -227,7 +231,7 @@
             carry = jnp.where(ahead, decay_span * carry + all_ref[other].astype(f32), carry)
         steps = (SUBS - 1 - sub if backward else sub).astype(f32)
         return tuple(
-            pre[m] + jnp.exp(-step_len * steps * spread(rate, m)) * spread(carry, m)
+            jnp.exp(-step_len * steps * spread(rate, m)) * spread(carry, m)
             for m in range(MODES)
         )
 
@@ -248,6 +252,15 @@
 
         lax.fori_loop(0, step_len, body, state, unroll=4)
 
+    def add_carried(out, state, backward):
+        def body(s, state):
+            t = step_len - 1 - s if backward else s
+            state = tuple(decays[m] * state[m] for m in range(MODES))
+            out[at_step(t), :] += tree(list(state))
+            return state
+
+        lax.fori_loop(0, step_len, body, tuple(gains[m] * state[m] for m in range(MODES)), unroll=4)
+
     def to_z(ref, units):
         batch = Batch(out_zs)
         for d in z_order:
@@ -265,27 +278,34 @@
     gates_in = Batch(out_x)
     for d in g_order:
         gates_in.send(gate_ref.at[:, lane(kp[d])], gateg.at[row(k), :], x_peer(d, 0), block_u)
+    signals.wait()
+    x_f[...] = xg[...].astype(f32)
+    prefix(ends(x_f, False), pre_f, False, e_all)
+    e_batch = to_z(e_all, 1)
     cot_a.wait()
-    for dy in y_order:
+    for dy in (1, -1):
         for d in (1, 2, 3):
             piece = (row(kp[d]), lane(j))
             cot_y[1].send(cotall.at[piece], cotall.at[piece], y_peer(dy), block_u)
-    signals.wait()
     weight_hop(2, 1)
-    x_f[...] = xg[...].astype(f32)
-    prefix(ends(x_f, False), pre_f, False, e_all)
-    e_batch = to_z(e_all, 1)
     cot_b.wait()
     other = (slice(None), lane(y * PAIR + xp[1]))
-    for dy in y_order:
+    for dy in (1, -1):
         cot_y[2].send(cotall.at[other], cotall.at[other], y_peer(dy), 4 * block_u)
+    cot_two.wait()
+    cot_spread = Batch(out_x)
+    j_two = lane(ymod(2) * PAIR + xl)
+    for dk, dx in x_order:
+        cot_spread.send(
+            two_ref.at[:, lane(kp[dk])], cotall.at[row(k), j_two], x_peer(dk, dx), block_u
+        )
+    cotall[row(k), j_two] = two_ref[:, lane(k)]
+    sweep(x_f, co_f, tuple(pre_f[m] for m in range(MODES)), False)
     weight_hop(3, 0)
     weight_hop(3, 1)
     e_batch.wait()
-    start_f = carried(pre_f, e_all, False)
-    for m in range(MODES):
-        pre_f[m] = start_f[m]
-    sweep(x_f, co_f, start_f, False)
+    start_f = carried(e_all, False)
+    add_carried(co_f, start_f, False)
     gates_in.wait()
     mixed_all[:, lane(k)] = (gateg[...].astype(f32) * co_f[...]).astype(bf16)
     mix_2 = Batch(out_x)
@@ -293,52 +313,67 @@
     mix_1 = Batch(out_x)
     mix_1.send(mixed_all.at[:, lane(k)], mixed_all.at[:, lane(k)], x_peer(1, 0), 4 * block_u)
     weight_hop(4, 0)
+    for m in range(MODES):
+        pre_f[m] += start_f[m]
     mix_2.wait()
     mix_1.send(mixed_all.at[:, lane(k2)], mixed_all.at[:, lane(k2)], x_peer(1, 0), 4 * block_u)
     weight_hop(4, 1)
     weight_hop(5, 0)
-    def out_grad_part(d):
+    side = span // 2
+    sides = [pl.ds(h * side, side) for h in (0, 1)]
+
+    def out_grad_part(h, d):
         return lax.dot_general(
-            cotall[:, pair(ymod(d))], wall[:, pair(ymod(d))], (((1,), (1,)), ((), ())),
+            cotall[sides[h], pair(ymod(d))], wall[:, pair(ymod(d))], (((1,), (1,)), ((), ())),
             preferred_element_type=f32,
         )
 
-    og_acc[...] = out_grad_part(0)
-    for batch in cot_y:
+    for h in (0, 1):
+        og_acc[sides[h], :] = out_grad_part(h, 0)
+    for batch in (*cot_y, cot_spread):
         batch.wait()
-    og_acc[...] += out_grad_part(1)
-    og_acc[...] += out_grad_part(-1)
-    og_acc[...] += out_grad_part(2)
-    og_a = Batch(out_x)
-    og_send[0] = og_acc[:, lane(k3)].astype(bf16)
-    og_a.send(og_send.at[0], og_recv.at[0], x_peer(1, 0), 4 * block_u)
+    og_a = [Batch(out_x), Batch(out_x)]
     og_b = Batch(out_x)
-    og_send[1] = og_acc[:, lane(k1)].astype(bf16)
-    og_b.send(og_send.at[1], og_recv.at[1], x_peer(1, 0), 4 * block_u)
+    for h in (0, 1):
+        for d in (1, -1, 2):
+            og_acc[sides[h], :] += out_grad_part(h, d)
+        og_send[0, sides[h], :] = og_acc[sides[h], lane(k3)].astype(bf16)
+        og_a[h].send(
+            og_send.at[0, sides[h]], og_recv.at[0, sides[h]], x_peer(1, 0), 2 * block_u
+        )
+        og_send[1, sides[h], :] = og_acc[sides[h], lane(k1)].astype(bf16)
+        og_b.send(
+            og_send.at[1, sides[h]], og_recv.at[1, sides[h]], x_peer(1, 0), 2 * block_u
+        )
 
     mix_1.wait()
 
-    for n in range(ys):
-        cols = slice(n * wide, (n + 1) * wide)
-        fp[:, cols] = jnp.dot(
-            mixed_all[...], wall[:, cols], preferred_element_type=f32
-        ).astype(bf16)
-    fin_batch = Batch(out_y)
-    for d in (1, -1, 2):
-        fin_batch.send(
-            fp.at[:, pair(ymod(d))], frecv.at[{1: 0, -1: 1, 2: 2}[d]], y_peer(d), 8 * block_u
-        )
-
-    og_a.wait()
-    og_send[2] = (og_acc[:, lane(k2)] + og_recv[0].astype(f32)).astype(bf16)
-    og_c = Batch(out_x)
-    og_c.send(og_send.at[2], og_recv.at[2], x_peer(2, 0), 4 * block_u)
-    for n in range(ys):
-        cols = slice(n * wide, (n + 1) * wide)
-        gp[:, cols] = lax.dot_general(
-            mixed_all[...], cotall[:, cols], (((0,), (0,)), ((), ())),
+    far_rows = pl.ds(pl.multiple_of((1 - lax.div(k, 2)) * side, side), side)
+    near_rows = pl.ds(pl.multiple_of(lax.div(k, 2) * side, side), side)
+    fin_parts = []
+
+    def output_part(part_rows):
+        for n in range(ys):
+            cols = slice(n * wide, (n + 1) * wide)
+            fp[part_rows, cols] = jnp.dot(
+                mixed_all[part_rows, :], wall[:, cols], preferred_element_type=f32
+            ).astype(bf16)
+        batch = Batch(out_y)
+        for d in y_order:
+            batch.send(
+                fp.at[part_rows, pair(ymod(d))],
+                frecv.at[{1: 0, -1: 1, 2: 2}[d], part_rows, :], y_peer(d), 4 * block_u,
+            )
+        fin_parts.append(batch)
+
+    output_part(far_rows)
+    def weight_term(d):
+        block = lane(zmod(d))
+        gp[:, block] = lax.dot_general(
+            mixed_all[...], cotall[:, block], (((0,), (0,)), ((), ())),
             preferred_element_type=f32,
         ).astype(bf16)
+
     sums = {}
     slots = {}
     for h in range(1, zs // 2 + 1):
@@ -365,11 +400,25 @@
                 src = rsbuf.at[slot]
             sums[h, long].send(src, rsbuf.at[slots[d, c, h]], z_peer(d), chunk_u)
 
+    weight_term(zs // 2)
     weight_sum_hop(1, 0)
+    og_c = Batch(out_x)
+    for h in (0, 1):
+        og_a[h].wait()
+        og_send[2, sides[h], :] = (
+            og_acc[sides[h], lane(k2)] + og_recv[0, sides[h], :].astype(f32)
+        ).astype(bf16)
+        og_c.send(
+            og_send.at[2, sides[h]], og_recv.at[2, sides[h]], x_peer(2, 0), 2 * block_u
+        )
+    output_part(near_rows)
+    weight_term(zs // 2 - 1)
+    weight_term(1 - zs // 2)
     weight_sum_hop(1, 1)
+    for d in range(2 - zs // 2, zs // 2 - 1):
+        weight_term(d)
     weight_sum_hop(2, 0)
 
-    weight_sum_hop(2, 1)
     og_b.wait()
     og_c.wait()
     og = og_acc[:, lane(k)] + og_recv[1].astype(f32) + og_recv[2].astype(f32)
@@ -377,6 +426,7 @@
     cg_f[...] = og * gateg[...].astype(f32)
     prefix(ends(cg_f, True), pre_b, True, b_all)
     b_batch = to_z(b_all, 1)
+    weight_sum_hop(2, 1)
     gates_g[...] = (og * co_f[...]).astype(bf16)
     gate_batch = Batch(out_x)
     for d in g_order:
@@ -395,42 +445,54 @@
         (tuple(pre_f[m] for m in range(MODES)), (zero,) * MODES), unroll=4,
     )
     for m in range(MODES):
-        l_all[z, m : m + 1, :] = jnp.sum(mode_sums[m], axis=0, keepdims=True)
-    l_all[z, MODES : MODES + 8, :] = jnp.broadcast_to(
-        jnp.sum(cg_f[...] * x_f[...], axis=0, keepdims=True), (8, LANES)
+        l_s[m : m + 1, :] = jnp.sum(mode_sums[m], axis=0, keepdims=True)
+    skip_sum = jnp.broadcast_to(
+        jnp.sum(cg_f[...] * x_f[...], axis=0, keepdims=True), (SUBS, LANES)
     )
-    l_batch = to_z(l_all, 3)
+    skip_high = skip_sum.astype(bf16).astype(f32)
+    l_s[MODES : MODES + SUBS, :] = skip_high
+    l_s[MODES + SUBS : MODES + 2 * SUBS, :] = skip_sum - skip_high
+    l_all[z] = l_s[...].astype(bf16)
     weight_sum_hop(3, 0)
 
-    weight_sum_hop(3, 1)
+    l_batch = to_z(l_all, 2)
+    sweep(cg_f, co_f, tuple(pre_b[m] for m in range(MODES)), True)
+    out_batch = Batch(out_x)
+
+    def finish(batch, part_rows, order):
+        batch.wait()
+        fin = fp[part_rows, pair(y)].astype(f32)
+        for n in range(ys - 1):
+            fin = fin + frecv[n, part_rows, :].astype(f32)
+        fin_y[part_rows, :] = fin.astype(bf16)
+        for dk, dx in order:
+            out_batch.send(
+                fin_y.at[row(kp[dk]), lane(xp[dx])], fin_pos.at[xl, :, lane(k)],
+                x_peer(dk, dx), block_u,
+            )
+
+    finish(fin_parts[0], far_rows, [(dk, dx) for dk in (2, 3) for dx in (1, 0)])
     b_batch.wait()
-    sweep(cg_f, co_f, carried(pre_b, b_all, True), True)
+    add_carried(co_f, carried(b_all, True), True)
     ggrp[...] = co_f[...].astype(bf16)
     gg_batch = Batch(out_x)
     for d in g_order:
         gg_batch.send(ggrp.at[row(kp[d]), :], ggpos.at[:, lane(k)], x_peer(d, 0), block_u)
     ggpos[:, lane(k)] = ggrp[row(k), :]
+    weight_sum_hop(3, 1)
+    finish(fin_parts[1], near_rows, [(0, 1), (1, 1), (1, 0)])
+    fin_pos[xl, :, lane(k)] = fin_y[row(k), lane(xl)]
+
     weight_sum_hop(4, 0)
 
-    fin_batch.wait()
-    fin = fp[:, pair(y)].astype(f32)
-    for n in range(ys - 1):
-        fin = fin + frecv[n].astype(f32)
-    fin_y[...] = fin.astype(bf16)
-    out_batch = Batch(out_x)
-    for dk, dx in x_order:
-        out_batch.send(
-            fin_y.at[row(kp[dk]), lane(xp[dx])], fin_pos.at[xl, :, lane(k)],
-            x_peer(dk, dx), block_u,
-        )
-    fin_pos[xl, :, lane(k)] = fin_y[row(k), lane(xl)]
-
     l_batch.wait()
-    total = l_all[0]
+    total = l_all[0].astype(f32)
     for n in range(1, zs):
-        total = total + l_all[n]
+        total = total + l_all[n].astype(f32)
     tot_all[0:MODES, lane(k)] = total[0:MODES] * inv_norm * scale
-    tot_all[MODES : MODES + 8, lane(k)] = total[MODES : MODES + 8] * scale
+    tot_all[MODES : MODES + SUBS, lane(k)] = (
+        total[MODES : MODES + SUBS] + total[MODES + SUBS : MODES + 2 * SUBS]
+    ) * scale
     tot_batch = Batch(out_zs)
     for d in g_order:
         tot_batch.send(tot_all.at[:, lane(k)], tot_all.at[:, lane(k)], x_peer(d, 0), 3)
@@ -471,6 +533,7 @@
         out.wait()
     for copy in writes:
         copy.wait()
+    assert counts == [RECEIVES, SENDS], counts
 
 
 def store_kernel(*refs):
@@ -522,6 +585,7 @@
             pltpu.VMEM((MODES, width), f32),
             pltpu.VMEM((1, width), f32),
             pltpu.VMEM((rows, width), bf16),
+            pltpu.VMEM((rows, width), bf16),
             pltpu.VMEM((span, columns), bf16),
             pltpu.VMEM((depth, columns), bf16),
             pltpu.VMEM((span, LANES), bf16),
@@ -534,7 +598,8 @@
             pltpu.VMEM((zs, MODES, LANES), bf16),
             pltpu.VMEM((zs, MODES, LANES), bf16),
             pltpu.VMEM((MODES, LANES), f32),
-            pltpu.VMEM((zs, MODES + 8, LANES), f32),
+            pltpu.VMEM((MODES + 2 * SUBS, LANES), f32),
+            pltpu.VMEM((zs, MODES + 2 * SUBS, LANES), bf16),
             pltpu.VMEM((span, width), bf16),
             pltpu.VMEM((span, width), f32),
             pltpu.VMEM((3, span, LANES), bf16),
@@ -551,8 +616,8 @@
             pltpu.VMEM((MODES + 8, width), f32),
             pltpu.VMEM((512, 16, LANES), bf16),
             *[pltpu.VMEM(a.shape, a.dtype) for a in out_shape[:5]],
-            pltpu.SemaphoreType.DMA((36,)),
-            pltpu.SemaphoreType.DMA((6,)),
+            pltpu.SemaphoreType.DMA((RECEIVES,)),
+            pltpu.SemaphoreType.DMA((SENDS,)),
             pltpu.SemaphoreType.DMA((8,)),
         ],
         compiler_params=pltpu.CompilerParams(

time: 54.3 us -> 50.4 us (0.928)
  Pallas kernels: 53.5 us -> 49.6 us
    pallas_call x1, Pallas kernels: 51.6 us -> 47.7 us  [shards(): pl.pallas_call(functools.partial(kernel, zs, chans, length), out_shape=ou...]
where the time goes in v4:
time: 50.4 us; the launch traced here: 50.3 us
  Pallas kernels  49.6 us (98%)
  between operations  0.64 us (1%)
    pallas_call x1, Pallas kernels, shards(): pl.pallas_call(functools.partial(kernel, zs, chans, length), out_shape=ou...  47.7 us
    pallas_call x1, Pallas kernels, shards(): pl.pallas_call(store_kernel, out_shape=out_shape, in_specs=[hbm] * 7, out...  1.95 us

profile of v4, /device:TPU:1, one launch (start us, length us, event | category | flops | bytes accessed | tf_op | source)
XLA Modules:
  0.0 50.3 jit_solution(208792882865059579)
XLA Ops:
  0.6 47.7 %shard_map.135 = (bf16[128,512]{1,0:T(8,128)(2,1)}, bf16[128,512]{1,0:T(8,128)(2,1)}, bf16[128,512]{1,0:T(8,128)(2,1)}, bf16[128,512]{1,0:T(8,128)(2,1)}, bf16[5...) custom-call(bf16[128,512]{1,0:T(8,128)(2,1)} %q_hbm.1, bf16[128,512]{1,0:T(8,128)(2,1)} %key_hbm.1, ...), custom_call_target="tpu_custom_call" | custom-call | tf_op jit(solution)/shard_map/pallas_call | solution.py:573
  48.3 1.9 %shard_map.136 = (bf16[128,512]{1,0:T(8,128)(2,1)}, bf16[128,512]{1,0:T(8,128)(2,1)}, bf16[128,512]{1,0:T(8,128)(2,1)}, bf16[128,512]{1,0:T(8,128)(2,1)}, bf16[5...) custom-call(bf16[128,512]{1,0:T(8,128)(2,1)} %get-tuple-element.21.refs_0_, ...), custom_call_target="tpu_custom_call" | custom-call | tf_op jit(solution)/shard_map/pallas_call | solution.py:627

commit v5 on v4

--- a/solution.py
+++ b/solution.py
@@ -17,8 +17,8 @@
 LANES = 128
 SUBS = 8
 MODES = 16
-RECEIVES = 38
-SENDS = 6
+RECEIVES = 39
+SENDS = 7
 
 
 def one_minus_exp(x):
@@ -33,7 +33,7 @@
     q_hbm, key_hbm, gate_hbm, cot_hbm, w_hbm, rate_hbm, res_hbm, skip_hbm,
     final_hbm, gq_hbm, gk_hbm, gg_hbm, gw_hbm, gres_hbm, gskip_hbm,
     q_ref, key_ref, gate_ref, cot_ref, w_ref, rate_ref, res_ref, skip_ref,
-    gat_s, two_ref, cotall, wall, xg, gateg, x_f, co_f, cg_f, pre_f, pre_b, e_all, b_all, ends_s, l_s, l_all,
+    gat_s, two_ref, cotall, wall, xg, gateg, x_f, co_f, cg_f, pre_f, pre_b, e_all, b_all, ends_s, l_s, l_all, skip_all, sizes_one,
     mixed_all, og_acc, og_send, og_recv, fp, frecv, fin_y, fin_pos, gp, rsbuf,
     ggrp, ggpos, gates_g, tot_all, sizes,
     final_ref, gq_ref, gk_ref, gg_ref, gw_ref,
@@ -105,23 +105,25 @@
             self.out.units += units
 
         def wait(self):
-            part = sizes.at[pl.ds(0, self.units)]
+            part = self.out.sizes.at[pl.ds(0, self.units)]
             pltpu.make_async_copy(part, part, self.recv).wait()
 
     class Outgoing:
-        def __init__(self):
+        def __init__(self, size_ref=sizes):
+            self.sizes = size_ref
             self.sem = send_sems.at[counts[1]]
             counts[1] += 1
             self.units = 0
 
         def wait(self):
-            part = sizes.at[pl.ds(0, self.units)]
+            part = self.sizes.at[pl.ds(0, self.units)]
             pltpu.make_async_copy(part, part, self.sem).wait()
 
     block_u = rows // 16
     out_x, out_y, out_z, out_zs, out_s, first_z = (
         Outgoing() for _ in range(6)
     )
+    out_one = Outgoing(sizes_one)
 
     barrier = pltpu.get_barrier_semaphore()
     peers = [x_peer(*d) for d in x_order]
@@ -300,9 +302,8 @@
             two_ref.at[:, lane(kp[dk])], cotall.at[row(k), j_two], x_peer(dk, dx), block_u
         )
     cotall[row(k), j_two] = two_ref[:, lane(k)]
+    weight_hop(3, 0)
     sweep(x_f, co_f, tuple(pre_f[m] for m in range(MODES)), False)
-    weight_hop(3, 0)
-    weight_hop(3, 1)
     e_batch.wait()
     start_f = carried(e_all, False)
     add_carried(co_f, start_f, False)
@@ -312,6 +313,7 @@
     mix_2.send(mixed_all.at[:, lane(k)], mixed_all.at[:, lane(k)], x_peer(2, 0), 4 * block_u)
     mix_1 = Batch(out_x)
     mix_1.send(mixed_all.at[:, lane(k)], mixed_all.at[:, lane(k)], x_peer(1, 0), 4 * block_u)
+    weight_hop(3, 1)
     weight_hop(4, 0)
     for m in range(MODES):
         pre_f[m] += start_f[m]
@@ -366,7 +368,6 @@
             )
         fin_parts.append(batch)
 
-    output_part(far_rows)
     def weight_term(d):
         block = lane(zmod(d))
         gp[:, block] = lax.dot_general(
@@ -402,6 +403,7 @@
 
     weight_term(zs // 2)
     weight_sum_hop(1, 0)
+    output_part(far_rows)
     og_c = Batch(out_x)
     for h in (0, 1):
         og_a[h].wait()
@@ -446,16 +448,14 @@
     )
     for m in range(MODES):
         l_s[m : m + 1, :] = jnp.sum(mode_sums[m], axis=0, keepdims=True)
-    skip_sum = jnp.broadcast_to(
-        jnp.sum(cg_f[...] * x_f[...], axis=0, keepdims=True), (SUBS, LANES)
-    )
-    skip_high = skip_sum.astype(bf16).astype(f32)
-    l_s[MODES : MODES + SUBS, :] = skip_high
-    l_s[MODES + SUBS : MODES + 2 * SUBS, :] = skip_sum - skip_high
     l_all[z] = l_s[...].astype(bf16)
+    skip_all[z] = jnp.sum(cg_f[...] * x_f[...], axis=0, keepdims=True)
+    l_batch = to_z(l_all, 1)
+    skip_batch = Batch(out_one)
+    for d in z_order:
+        skip_batch.send(skip_all.at[z], skip_all.at[z], z_peer(d), 1)
     weight_sum_hop(3, 0)
 
-    l_batch = to_z(l_all, 2)
     sweep(cg_f, co_f, tuple(pre_b[m] for m in range(MODES)), True)
     out_batch = Batch(out_x)
 
@@ -480,22 +480,24 @@
         gg_batch.send(ggrp.at[row(kp[d]), :], ggpos.at[:, lane(k)], x_peer(d, 0), block_u)
     ggpos[:, lane(k)] = ggrp[row(k), :]
     weight_sum_hop(3, 1)
-    finish(fin_parts[1], near_rows, [(0, 1), (1, 1), (1, 0)])
-    fin_pos[xl, :, lane(k)] = fin_y[row(k), lane(xl)]
-
-    weight_sum_hop(4, 0)
-
     l_batch.wait()
+    skip_batch.wait()
     total = l_all[0].astype(f32)
     for n in range(1, zs):
         total = total + l_all[n].astype(f32)
     tot_all[0:MODES, lane(k)] = total[0:MODES] * inv_norm * scale
-    tot_all[MODES : MODES + SUBS, lane(k)] = (
-        total[MODES : MODES + SUBS] + total[MODES + SUBS : MODES + 2 * SUBS]
-    ) * scale
+    total = skip_all[0]
+    for n in range(1, zs):
+        total = total + skip_all[n]
+    tot_all[MODES : MODES + SUBS, lane(k)] = spread(total, 0) * scale
     tot_batch = Batch(out_zs)
     for d in g_order:
         tot_batch.send(tot_all.at[:, lane(k)], tot_all.at[:, lane(k)], x_peer(d, 0), 3)
+    finish(fin_parts[1], near_rows, [(0, 1), (1, 1), (1, 0)])
+    fin_pos[xl, :, lane(k)] = fin_y[row(k), lane(xl)]
+
+    weight_sum_hop(4, 0)
+
     writes = []
 
     def write(n, src, dst):
@@ -529,7 +531,7 @@
     out_batch.wait()
     final_ref[...] = (fin_pos[0].astype(f32) + fin_pos[1].astype(f32)).astype(bf16)
     write(0, final_ref, final_hbm)
-    for out in (out_x, out_y, out_z, out_zs, out_s):
+    for out in (out_x, out_y, out_z, out_zs, out_s, out_one):
         out.wait()
     for copy in writes:
         copy.wait()
@@ -598,8 +600,10 @@
             pltpu.VMEM((zs, MODES, LANES), bf16),
             pltpu.VMEM((zs, MODES, LANES), bf16),
             pltpu.VMEM((MODES, LANES), f32),
-            pltpu.VMEM((MODES + 2 * SUBS, LANES), f32),
-            pltpu.VMEM((zs, MODES + 2 * SUBS, LANES), bf16),
+            pltpu.VMEM((MODES, LANES), f32),
+            pltpu.VMEM((zs, MODES, LANES), bf16),
+            pltpu.VMEM((zs, 1, LANES), f32),
+            pltpu.VMEM((zs, 1, LANES), f32),
             pltpu.VMEM((span, width), bf16),
             pltpu.VMEM((span, width), f32),
             pltpu.VMEM((3, span, LANES), bf16),

time: 50.4 us -> 49.7 us (0.986)
  Pallas kernels: 49.6 us -> 48.9 us
    pallas_call x1, Pallas kernels: 47.7 us -> 47 us  [shards(): pl.pallas_call(functools.partial(kernel, zs, chans, length), out_shape=ou...]
where the time goes in v5:
time: 49.7 us; the launch traced here: 49.6 us
  Pallas kernels  48.9 us (98%)
  between operations  0.64 us (1%)
    pallas_call x1, Pallas kernels, shards(): pl.pallas_call(functools.partial(kernel, zs, chans, length), out_shape=ou...  47 us
    pallas_call x1, Pallas kernels, shards(): pl.pallas_call(store_kernel, out_shape=out_shape, in_specs=[hbm] * 7, out...  1.95 us

profile of v5, /device:TPU:1, one launch (start us, length us, event | category | flops | bytes accessed | tf_op | source)
XLA Modules:
  0.0 49.6 jit_solution(1153383310233603521)
XLA Ops:
  0.6 47.0 %shard_map.135 = (bf16[128,512]{1,0:T(8,128)(2,1)}, bf16[128,512]{1,0:T(8,128)(2,1)}, bf16[128,512]{1,0:T(8,128)(2,1)}, bf16[128,512]{1,0:T(8,128)(2,1)}, bf16[5...) custom-call(bf16[128,512]{1,0:T(8,128)(2,1)} %q_hbm.1, bf16[128,512]{1,0:T(8,128)(2,1)} %key_hbm.1, ...), custom_call_target="tpu_custom_call" | custom-call | tf_op jit(solution)/shard_map/pallas_call | solution.py:575
  47.6 1.9 %shard_map.136 = (bf16[128,512]{1,0:T(8,128)(2,1)}, bf16[128,512]{1,0:T(8,128)(2,1)}, bf16[128,512]{1,0:T(8,128)(2,1)}, bf16[128,512]{1,0:T(8,128)(2,1)}, bf16[5...) custom-call(bf16[128,512]{1,0:T(8,128)(2,1)} %get-tuple-element.21.refs_0_, ...), custom_call_target="tpu_custom_call" | custom-call | tf_op jit(solution)/shard_map/pallas_call | solution.py:631

commit v6 on v5

--- a/solution.py
+++ b/solution.py
@@ -17,7 +17,7 @@
 LANES = 128
 SUBS = 8
 MODES = 16
-RECEIVES = 39
+RECEIVES = 53
 SENDS = 7
 
 
@@ -149,16 +149,20 @@
     ring = {}
     chunk_u = half // 16
 
+    def quarter(c, q):
+        return pl.ds(c * half + q * (half // 2), half // 2)
+
     def weight_hop(h, long):
-        if h > 1:
-            ring[h - 1, long].wait()
-        if h > ways[long][0][2]:
-            return
-        ring[h, long] = Batch(first_z if (h, long) == (1, 0) else out_z)
-        for d, c, hops in ways[long]:
-            block = lane(zmod(-d * (h - 1)))
-            src = w_hbm.at[chunk[c], :] if h == 1 else wall.at[chunk[c], block]
-            ring[h, long].send(src, wall.at[chunk[c], block], z_peer(d), chunk_u)
+        for q in (0, 1):
+            if h > 1:
+                ring[h - 1, long, q].wait()
+            if h > ways[long][0][2]:
+                continue
+            ring[h, long, q] = Batch(first_z if (h, long) == (1, 0) else out_z)
+            for d, c, hops in ways[long]:
+                spot = (quarter(c, q), lane(zmod(-d * (h - 1))))
+                src = w_hbm.at[spot[0], :] if h == 1 else wall.at[spot]
+                ring[h, long, q].send(src, wall.at[spot], z_peer(d), chunk_u // 2)
 
     y_order = (2, 1, -1)
     cot_y = [Batch(out_y) for _ in range(3)]
@@ -290,10 +294,6 @@
             piece = (row(kp[d]), lane(j))
             cot_y[1].send(cotall.at[piece], cotall.at[piece], y_peer(dy), block_u)
     weight_hop(2, 1)
-    cot_b.wait()
-    other = (slice(None), lane(y * PAIR + xp[1]))
-    for dy in (1, -1):
-        cot_y[2].send(cotall.at[other], cotall.at[other], y_peer(dy), 4 * block_u)
     cot_two.wait()
     cot_spread = Batch(out_x)
     j_two = lane(ymod(2) * PAIR + xl)
@@ -302,6 +302,10 @@
             two_ref.at[:, lane(kp[dk])], cotall.at[row(k), j_two], x_peer(dk, dx), block_u
         )
     cotall[row(k), j_two] = two_ref[:, lane(k)]
+    cot_b.wait()
+    other = (slice(None), lane(y * PAIR + xp[1]))
+    for dy in (1, -1):
+        cot_y[2].send(cotall.at[other], cotall.at[other], y_peer(dy), 4 * block_u)
     weight_hop(3, 0)
     sweep(x_f, co_f, tuple(pre_f[m] for m in range(MODES)), False)
     e_batch.wait()
@@ -368,6 +372,7 @@
             )
         fin_parts.append(batch)
 
+    output_part(far_rows)
     def weight_term(d):
         block = lane(zmod(d))
         gp[:, block] = lax.dot_general(
@@ -384,26 +389,29 @@
                     slots[d, c, h] = len(slots)
 
     def weight_sum_hop(h, long):
-        if h > 1:
-            sums[h - 1, long].wait()
-        if h > ways[long][0][2]:
-            return
-        sums[h, long] = Batch(out_s)
-        for d, c, hops in ways[long]:
-            block = lane(zmod(d * (hops - h + 1)))
-            if h == 1:
-                src = gp.at[chunk[c], block]
-            else:
-                slot = slots[d, c, h - 1]
-                rsbuf[slot] = (
-                    rsbuf[slot].astype(f32) + gp[chunk[c], block].astype(f32)
-                ).astype(bf16)
-                src = rsbuf.at[slot]
-            sums[h, long].send(src, rsbuf.at[slots[d, c, h]], z_peer(d), chunk_u)
+        for q in (0, 1):
+            if h > 1:
+                sums[h - 1, long, q].wait()
+            if h > ways[long][0][2]:
+                continue
+            sums[h, long, q] = Batch(out_s)
+            part = pl.ds(q * (half // 2), half // 2)
+            for d, c, hops in ways[long]:
+                block = lane(zmod(d * (hops - h + 1)))
+                if h == 1:
+                    src = gp.at[quarter(c, q), block]
+                else:
+                    slot = slots[d, c, h - 1]
+                    rsbuf[slot, part, :] = (
+                        rsbuf[slot, part, :].astype(f32) + gp[quarter(c, q), block].astype(f32)
+                    ).astype(bf16)
+                    src = rsbuf.at[slot, part]
+                sums[h, long, q].send(
+                    src, rsbuf.at[slots[d, c, h], part], z_peer(d), chunk_u // 2
+                )
 
     weight_term(zs // 2)
     weight_sum_hop(1, 0)
-    output_part(far_rows)
     og_c = Batch(out_x)
     for h in (0, 1):
         og_a[h].wait()

time: 49.7 us -> 48.4 us (0.974)
  Pallas kernels: 48.9 us -> 47.7 us
    pallas_call x1, Pallas kernels: 47 us -> 45.8 us  [shards(): pl.pallas_call(functools.partial(kernel, zs, chans, length), out_shape=ou...]
where the time goes in v6:
time: 48.4 us; the launch traced here: 48.3 us
  Pallas kernels  47.7 us (99%)
  between operations  0.64 us (1%)
    pallas_call x1, Pallas kernels, shards(): pl.pallas_call(functools.partial(kernel, zs, chans, length), out_shape=ou...  45.8 us
    pallas_call x1, Pallas kernels, shards(): pl.pallas_call(store_kernel, out_shape=out_shape, in_specs=[hbm] * 7, out...  1.95 us

profile of v6, /device:TPU:1, one launch (start us, length us, event | category | flops | bytes accessed | tf_op | source)
XLA Modules:
  0.0 48.3 jit_solution(7744195841299035664)
XLA Ops:
  0.6 45.8 %shard_map.135 = (bf16[128,512]{1,0:T(8,128)(2,1)}, bf16[128,512]{1,0:T(8,128)(2,1)}, bf16[128,512]{1,0:T(8,128)(2,1)}, bf16[128,512]{1,0:T(8,128)(2,1)}, bf16[5...) custom-call(bf16[128,512]{1,0:T(8,128)(2,1)} %q_hbm.1, bf16[128,512]{1,0:T(8,128)(2,1)} %key_hbm.1, ...), custom_call_target="tpu_custom_call" | custom-call | tf_op jit(solution)/shard_map/pallas_call | solution.py:583
  46.4 1.9 %shard_map.136 = (bf16[128,512]{1,0:T(8,128)(2,1)}, bf16[128,512]{1,0:T(8,128)(2,1)}, bf16[128,512]{1,0:T(8,128)(2,1)}, bf16[128,512]{1,0:T(8,128)(2,1)}, bf16[5...) custom-call(bf16[128,512]{1,0:T(8,128)(2,1)} %get-tuple-element.21.refs_0_, ...), custom_call_target="tpu_custom_call" | custom-call | tf_op jit(solution)/shard_map/pallas_call | solution.py:639

commit v7 on v6

--- a/solution.py
+++ b/solution.py
@@ -212,7 +212,7 @@
             value = src[at_step(t), :]
             return tuple(decays[m] * state[m] + value for m in range(MODES))
 
-        return lax.fori_loop(0, step_len, body, (zero,) * MODES, unroll=4)
+        return lax.fori_loop(0, step_len, body, (zero,) * MODES, unroll=8)
 
     def prefix(state, pre, backward, all_ref):
         for m in range(MODES):
@@ -256,7 +256,7 @@
             )
             return state
 
-        lax.fori_loop(0, step_len, body, state, unroll=4)
+        lax.fori_loop(0, step_len, body, state, unroll=8)
 
     def add_carried(out, state, backward):
         def body(s, state):
@@ -265,7 +265,7 @@
             out[at_step(t), :] += tree(list(state))
             return state
 
-        lax.fori_loop(0, step_len, body, tuple(gains[m] * state[m] for m in range(MODES)), unroll=4)
+        lax.fori_loop(0, step_len, body, tuple(gains[m] * state[m] for m in range(MODES)), unroll=8)
 
     def to_z(ref, units):
         batch = Batch(out_zs)
@@ -321,28 +321,33 @@
     weight_hop(4, 0)
     for m in range(MODES):
         pre_f[m] += start_f[m]
+    side = span // 2
+    sides = [pl.ds(h * side, side) for h in (0, 1)]
+
+    def add_out_grad(h, steps):
+        for d in steps:
+            block = lane(zmod(d))
+            part = lax.dot_general(
+                cotall[sides[h], block], wall[:, block], (((1,), (1,)), ((), ())),
+                preferred_element_type=f32,
+            )
+            if d == 0:
+                og_acc[sides[h], :] = part
+            else:
+                og_acc[sides[h], :] += part
+
+    for batch in (*cot_y, cot_spread):
+        batch.wait()
+    for h in (0, 1):
+        add_out_grad(h, (0, 1, -1, 2, -2))
     mix_2.wait()
     mix_1.send(mixed_all.at[:, lane(k2)], mixed_all.at[:, lane(k2)], x_peer(1, 0), 4 * block_u)
     weight_hop(4, 1)
     weight_hop(5, 0)
-    side = span // 2
-    sides = [pl.ds(h * side, side) for h in (0, 1)]
-
-    def out_grad_part(h, d):
-        return lax.dot_general(
-            cotall[sides[h], pair(ymod(d))], wall[:, pair(ymod(d))], (((1,), (1,)), ((), ())),
-            preferred_element_type=f32,
-        )
-
-    for h in (0, 1):
-        og_acc[sides[h], :] = out_grad_part(h, 0)
-    for batch in (*cot_y, cot_spread):
-        batch.wait()
     og_a = [Batch(out_x), Batch(out_x)]
     og_b = Batch(out_x)
     for h in (0, 1):
-        for d in (1, -1, 2):
-            og_acc[sides[h], :] += out_grad_part(h, d)
+        add_out_grad(h, (zs // 2 - 1, 1 - zs // 2, zs // 2))
         og_send[0, sides[h], :] = og_acc[sides[h], lane(k3)].astype(bf16)
         og_a[h].send(
             og_send.at[0, sides[h]], og_recv.at[0, sides[h]], x_peer(1, 0), 2 * block_u
@@ -421,10 +426,10 @@
         og_c.send(
             og_send.at[2, sides[h]], og_recv.at[2, sides[h]], x_peer(2, 0), 2 * block_u
         )
-    output_part(near_rows)
     weight_term(zs // 2 - 1)
     weight_term(1 - zs // 2)
     weight_sum_hop(1, 1)
+    output_part(near_rows)
     for d in range(2 - zs // 2, zs // 2 - 1):
         weight_term(d)
     weight_sum_hop(2, 0)
@@ -452,7 +457,7 @@
 
     _, mode_sums = lax.fori_loop(
         0, step_len, residue_body,
-        (tuple(pre_f[m] for m in range(MODES)), (zero,) * MODES), unroll=4,
+        (tuple(pre_f[m] for m in range(MODES)), (zero,) * MODES), unroll=8,
     )
     for m in range(MODES):
         l_s[m : m + 1, :] = jnp.sum(mode_sums[m], axis=0, keepdims=True)
@@ -488,6 +493,8 @@
         gg_batch.send(ggrp.at[row(kp[d]), :], ggpos.at[:, lane(k)], x_peer(d, 0), block_u)
     ggpos[:, lane(k)] = ggrp[row(k), :]
     weight_sum_hop(3, 1)
+    weight_sum_hop(4, 0)
+
     l_batch.wait()
     skip_batch.wait()
     total = l_all[0].astype(f32)
@@ -503,8 +510,6 @@
         tot_batch.send(tot_all.at[:, lane(k)], tot_all.at[:, lane(k)], x_peer(d, 0), 3)
     finish(fin_parts[1], near_rows, [(0, 1), (1, 1), (1, 0)])
     fin_pos[xl, :, lane(k)] = fin_y[row(k), lane(xl)]
-
-    weight_sum_hop(4, 0)
 
     writes = []
 

time: 48.4 us -> 48.1 us (level)
  no operation moved by 1% of the time
where the time goes in v7:
time: 48.1 us; the launch traced here: 48 us
  Pallas kernels  47.3 us (98%)
  between operations  0.64 us (1%)
    pallas_call x1, Pallas kernels, shards(): pl.pallas_call(functools.partial(kernel, zs, chans, length), out_shape=ou...  45.4 us
    pallas_call x1, Pallas kernels, shards(): pl.pallas_call(store_kernel, out_shape=out_shape, in_specs=[hbm] * 7, out...  1.95 us

profile of v7, /device:TPU:1, one launch (start us, length us, event | category | flops | bytes accessed | tf_op | source)
XLA Modules:
  0.0 48.0 jit_solution(6555247981399426716)
XLA Ops:
  0.6 45.4 %shard_map.135 = (bf16[128,512]{1,0:T(8,128)(2,1)}, bf16[128,512]{1,0:T(8,128)(2,1)}, bf16[128,512]{1,0:T(8,128)(2,1)}, bf16[128,512]{1,0:T(8,128)(2,1)}, bf16[5...) custom-call(bf16[128,512]{1,0:T(8,128)(2,1)} %q_hbm.1, bf16[128,512]{1,0:T(8,128)(2,1)} %key_hbm.1, ...), custom_call_target="tpu_custom_call" | custom-call | tf_op jit(solution)/shard_map/pallas_call | solution.py:588
  46.0 1.9 %shard_map.136 = (bf16[128,512]{1,0:T(8,128)(2,1)}, bf16[128,512]{1,0:T(8,128)(2,1)}, bf16[128,512]{1,0:T(8,128)(2,1)}, bf16[128,512]{1,0:T(8,128)(2,1)}, bf16[5...) custom-call(bf16[128,512]{1,0:T(8,128)(2,1)} %get-tuple-element.21.refs_0_, ...), custom_call_target="tpu_custom_call" | custom-call | tf_op jit(solution)/shard_map/pallas_call | solution.py:644

commit v8 on v7

--- a/solution.py
+++ b/solution.py
@@ -17,7 +17,7 @@
 LANES = 128
 SUBS = 8
 MODES = 16
-RECEIVES = 53
+RECEIVES = 52
 SENDS = 7
 
 
@@ -417,13 +417,12 @@
 
     weight_term(zs // 2)
     weight_sum_hop(1, 0)
-    og_c = Batch(out_x)
     for h in (0, 1):
         og_a[h].wait()
         og_send[2, sides[h], :] = (
             og_acc[sides[h], lane(k2)] + og_recv[0, sides[h], :].astype(f32)
         ).astype(bf16)
-        og_c.send(
+        og_b.send(
             og_send.at[2, sides[h]], og_recv.at[2, sides[h]], x_peer(2, 0), 2 * block_u
         )
     weight_term(zs // 2 - 1)
@@ -435,7 +434,6 @@
     weight_sum_hop(2, 0)
 
     og_b.wait()
-    og_c.wait()
     og = og_acc[:, lane(k)] + og_recv[1].astype(f32) + og_recv[2].astype(f32)
     og = og.astype(bf16).astype(f32)
     cg_f[...] = og * gateg[...].astype(f32)
@@ -443,9 +441,9 @@
     b_batch = to_z(b_all, 1)
     weight_sum_hop(2, 1)
     gates_g[...] = (og * co_f[...]).astype(bf16)
-    gate_batch = Batch(out_x)
+    gg_batch = Batch(out_x)
     for d in g_order:
-        gate_batch.send(gates_g.at[row(kp[d]), :], gg_ref.at[:, lane(k)], x_peer(d, 0), block_u)
+        gg_batch.send(gates_g.at[row(kp[d]), :], gg_ref.at[:, lane(k)], x_peer(d, 0), block_u)
     gg_ref[:, lane(k)] = gates_g[row(k), :]
 
     def residue_body(s, carry):
@@ -470,9 +468,9 @@
     weight_sum_hop(3, 0)
 
     sweep(cg_f, co_f, tuple(pre_b[m] for m in range(MODES)), True)
-    out_batch = Batch(out_x)
-
-    def finish(batch, part_rows, order):
+    out_far, out_near = Batch(out_x), Batch(out_x)
+
+    def finish(batch, part_rows, order, out_batch):
         batch.wait()
         fin = fp[part_rows, pair(y)].astype(f32)
         for n in range(ys - 1):
@@ -484,11 +482,10 @@
                 x_peer(dk, dx), block_u,
             )
 
-    finish(fin_parts[0], far_rows, [(dk, dx) for dk in (2, 3) for dx in (1, 0)])
+    finish(fin_parts[0], far_rows, [(dk, dx) for dk in (2, 3) for dx in (1, 0)], out_far)
     b_batch.wait()
     add_carried(co_f, carried(b_all, True), True)
     ggrp[...] = co_f[...].astype(bf16)
-    gg_batch = Batch(out_x)
     for d in g_order:
         gg_batch.send(ggrp.at[row(kp[d]), :], ggpos.at[:, lane(k)], x_peer(d, 0), block_u)
     ggpos[:, lane(k)] = ggrp[row(k), :]
@@ -508,7 +505,7 @@
     tot_batch = Batch(out_zs)
     for d in g_order:
         tot_batch.send(tot_all.at[:, lane(k)], tot_all.at[:, lane(k)], x_peer(d, 0), 3)
-    finish(fin_parts[1], near_rows, [(0, 1), (1, 1), (1, 0)])
+    finish(fin_parts[1], near_rows, [(0, 1), (1, 1), (1, 0)], out_near)
     fin_pos[xl, :, lane(k)] = fin_y[row(k), lane(xl)]
 
     writes = []
@@ -524,7 +521,6 @@
     gk_ref[...] = (spread_grad * q_ref[...].astype(f32)).astype(bf16)
     write(1, gq_ref, gq_hbm)
     write(2, gk_ref, gk_hbm)
-    gate_batch.wait()
     write(3, gg_ref, gg_hbm)
 
     weight_sum_hop(4, 1)
@@ -541,9 +537,16 @@
     tot_batch.wait()
     write(5, tot_all.at[pl.ds(0, MODES), :], gres_hbm)
     write(6, tot_all.at[pl.ds(MODES, 1), :], gskip_hbm)
-    out_batch.wait()
-    final_ref[...] = (fin_pos[0].astype(f32) + fin_pos[1].astype(f32)).astype(bf16)
-    write(0, final_ref, final_hbm)
+    def write_output(n, batch, block):
+        batch.wait()
+        spot = (slice(None), pair(block))
+        final_ref[spot] = (
+            fin_pos[0, :, pair(block)].astype(f32) + fin_pos[1, :, pair(block)].astype(f32)
+        ).astype(bf16)
+        write(n, final_ref.at[spot], final_hbm.at[spot])
+
+    write_output(7, out_far, 1 - lax.div(k, 2))
+    write_output(0, out_near, lax.div(k, 2))
     for out in (out_x, out_y, out_z, out_zs, out_s, out_one):
         out.wait()
     for copy in writes:

time: 48.1 us -> 48.1 us (level)
  no operation moved by 1% of the time
where the time goes in v8:
time: 48.1 us; the launch traced here: 47.9 us
  Pallas kernels  47.3 us (98%)
  between operations  0.64 us (1%)
    pallas_call x1, Pallas kernels, shards(): pl.pallas_call(functools.partial(kernel, zs, chans, length), out_shape=ou...  45.4 us
    pallas_call x1, Pallas kernels, shards(): pl.pallas_call(store_kernel, out_shape=out_shape, in_specs=[hbm] * 7, out...  1.95 us

profile of v8, /device:TPU:1, one launch (start us, length us, event | category | flops | bytes accessed | tf_op | source)
XLA Modules:
  0.0 47.9 jit_solution(9649193841642087481)
XLA Ops:
  0.6 45.4 %shard_map.135 = (bf16[128,512]{1,0:T(8,128)(2,1)}, bf16[128,512]{1,0:T(8,128)(2,1)}, bf16[128,512]{1,0:T(8,128)(2,1)}, bf16[128,512]{1,0:T(8,128)(2,1)}, bf16[5...) custom-call(bf16[128,512]{1,0:T(8,128)(2,1)} %q_hbm.1, bf16[128,512]{1,0:T(8,128)(2,1)} %key_hbm.1, ...), custom_call_target="tpu_custom_call" | custom-call | tf_op jit(solution)/shard_map/pallas_call | solution.py:591
  46.0 1.9 %shard_map.136 = (bf16[128,512]{1,0:T(8,128)(2,1)}, bf16[128,512]{1,0:T(8,128)(2,1)}, bf16[128,512]{1,0:T(8,128)(2,1)}, bf16[128,512]{1,0:T(8,128)(2,1)}, bf16[5...) custom-call(bf16[128,512]{1,0:T(8,128)(2,1)} %get-tuple-element.21.refs_0_, ...), custom_call_target="tpu_custom_call" | custom-call | tf_op jit(solution)/shard_map/pallas_call | solution.py:647

commit v9 on v7

--- a/solution.py
+++ b/solution.py
@@ -135,7 +135,7 @@
     loads = [
         pltpu.make_async_copy(src, dst, load_sems.at[n])
         for n, (src, dst) in enumerate((
-            (cot_hbm, cot_ref), (w_hbm, w_ref), (q_hbm, q_ref), (key_hbm, key_ref),
+            (q_hbm, q_ref), (key_hbm, key_ref), (cot_hbm, cot_ref), (w_hbm, w_ref),
             (gate_hbm, gate_ref), (rate_hbm, rate_ref), (res_hbm, res_ref), (skip_hbm, skip_ref),
         ))
     ]
@@ -171,7 +171,7 @@
     cot_two = Batch(out_y)
     cot_two.send(cot_hbm, two_ref, y_peer(2), 4 * block_u)
     weight_hop(1, 0)
-    for copy in loads:
+    for copy in loads[:2]:
         copy.wait()
     gat_s[...] = (q_ref[...].astype(f32) * key_ref[...].astype(f32)).astype(bf16)
     signals = Batch(out_x)
@@ -182,6 +182,8 @@
         cot_a.send(
             cot_hbm.at[:, lane(kp[d])], cotall.at[row(k), lane(j)], x_peer(d, 0), block_u
         )
+    for copy in loads[2:]:
+        copy.wait()
     cotall[row(k), lane(j)] = cot_ref[:, lane(k)]
     xg[row(k), :] = gat_s[:, lane(k)]
     gateg[row(k), :] = gate_ref[:, lane(k)]

time: 48.1 us -> 48.1 us (level)
  no operation moved by 1% of the time
where the time goes in v9:
time: 48.1 us; the launch traced here: 48 us
  Pallas kernels  47.4 us (99%)
  between operations  0.64 us (1%)
    pallas_call x1, Pallas kernels, shards(): pl.pallas_call(functools.partial(kernel, zs, chans, length), out_shape=ou...  45.4 us
    pallas_call x1, Pallas kernels, shards(): pl.pallas_call(store_kernel, out_shape=out_shape, in_specs=[hbm] * 7, out...  1.95 us

profile of v9, /device:TPU:1, one launch (start us, length us, event | category | flops | bytes accessed | tf_op | source)
XLA Modules:
  0.0 48.0 jit_solution(14007553735118669759)
XLA Ops:
  0.6 45.4 %shard_map.135 = (bf16[128,512]{1,0:T(8,128)(2,1)}, bf16[128,512]{1,0:T(8,128)(2,1)}, bf16[128,512]{1,0:T(8,128)(2,1)}, bf16[128,512]{1,0:T(8,128)(2,1)}, bf16[5...) custom-call(bf16[128,512]{1,0:T(8,128)(2,1)} %q_hbm.1, bf16[128,512]{1,0:T(8,128)(2,1)} %key_hbm.1, ...), custom_call_target="tpu_custom_call" | custom-call | tf_op jit(solution)/shard_map/pallas_call | solution.py:590
  46.0 1.9 %shard_map.136 = (bf16[128,512]{1,0:T(8,128)(2,1)}, bf16[128,512]{1,0:T(8,128)(2,1)}, bf16[128,512]{1,0:T(8,128)(2,1)}, bf16[128,512]{1,0:T(8,128)(2,1)}, bf16[5...) custom-call(bf16[128,512]{1,0:T(8,128)(2,1)} %get-tuple-element.21.refs_0_, ...), custom_call_target="tpu_custom_call" | custom-call | tf_op jit(solution)/shard_map/pallas_call | solution.py:646
